TPU v7x, 256 devices: a whole 4x4x8 slice. The times are simulated.
256 devices in a mesh: seq: 64 (over y, z, core), head: 4 (over x).
Axes of the slice: x: 4, y: 4, z: 8, core: 2. Of those that a mesh axis runs over, the one named last changes fastest.
Arguments:
- query_rows: bfloat16 [65536, 1024], P('seq', 'head'), may hold values from -150 to 150
- key_rows: bfloat16 [65536, 1024], P('seq', 'head'), may hold values from -150 to 150
- value_rows: bfloat16 [65536, 1024], P('seq', 'head'), may hold values from -8 to 8
- segment: int32 [65536], P('seq'), may hold values from 0 to 254, as said below
- w_out: bfloat16 [1024, 1024], P('head'), may hold values from -0.5 to 0.5
Outputs:
- projected: bfloat16 [65536, 1024], P(('seq', 'head'))
Inputs may be any that keep to these rules, and one draw needn't show every extreme that they name: segment ids never fall along the sequence; each segment has 1 to 512 tokens, one of them exactly 512.
All inputs are finite; a program needn't handle non-finite values.
Results may differ from a plain program's by a relative error of at most 0.0069.
Values may be sent and summed in bfloat16 or wider, within the bound.
A program may use at most 128 MiB of HBM per device.

v0:
```python
import jax
import jax.numpy as jnp
from jax import lax
from jax.sharding import PartitionSpec as P

HEAD_DIM = 64
BLOCK = 256
LEVELS = 6


NEG_FILL = -1e30


def with_halo(array, sides, width):
    for axis, dim in sides:
        size, length = (lax.axis_size(axis), array.shape[dim])
        up = [(i, (i + 1) % size) for i in range(size - 1)]
        down = [(j, i) for i, j in up]
        last = lax.slice_in_dim(array, length - width, length, axis=dim)
        initial = lax.slice_in_dim(array, 0, width, axis=dim)
        before = lax.ppermute(last, axis, up)
        after = lax.ppermute(initial, axis, down)
        array = jnp.concatenate([before, array, after], axis=dim)
    return array


def from_behind(array, axis, by):
    length = lax.axis_size(axis)
    pairs = [(i, i + by) for i in range(length) if 0 <= i + by < length]
    return lax.ppermute(array, axis, pairs)


def block_attend(queries, key_block, value_block, allowed, scaling):
    scores = (
        jnp.einsum("nqhd,nkhd->nhqk", queries, key_block, preferred_element_type=jnp.float32)
        * scaling
    )
    mask_full = allowed[:, None]
    scores = jnp.where(mask_full, scores, NEG_FILL)
    peaks = jnp.max(scores, axis=-1)
    weights = jnp.where(mask_full, jnp.exp(scores - peaks[..., None]), 0.0)
    totals = jnp.sum(weights, axis=-1)
    weighted = jnp.einsum(
        "nhqk,nkhd->nqhd",
        weights.astype(jnp.bfloat16),
        value_block,
        preferred_element_type=jnp.float32,
    )
    return (jnp.swapaxes(peaks, 1, 2), jnp.swapaxes(totals, 1, 2), weighted)


def grouped_attend(queries, key_block, value_block, allowed, scaling):
    block_count = queries.shape[0]
    group_size = min(block_count, 2)
    if group_size == block_count:
        return block_attend(queries, key_block, value_block, allowed, scaling)

    def single_group(pieces):
        return block_attend(pieces[0], pieces[1], pieces[2], pieces[3], scaling)

    shaped = tuple(
        (
            source.reshape((block_count // group_size, group_size) + source.shape[1:])
            for source in (queries, key_block, value_block, allowed)
        )
    )
    peaks, totals, weighted = lax.map(single_group, shaped)
    return (
        peaks.reshape((block_count,) + peaks.shape[2:]),
        totals.reshape((block_count,) + totals.shape[2:]),
        weighted.reshape((block_count,) + weighted.shape[2:]),
    )


def on_device(query_rows, key_rows, value_rows, segment, w_out):
    tok_count, feat_count = query_rows.shape
    head_count = feat_count // HEAD_DIM
    scaling = HEAD_DIM ** (-0.5)
    seq_count = lax.axis_size("seq")
    seq_place = lax.axis_index("seq")
    current = [source.astype(jnp.float32) for source in (query_rows, key_rows, value_rows)]
    coarse_q = []
    coarse_kv = []
    for lev_index in range(LEVELS):
        if lev_index > 0:
            half_rows = current[0].shape[0] // 2
            current = [
                jnp.mean(source.reshape(half_rows, 2, feat_count), axis=1) for source in current
            ]
        coarse_q.append(current[0].astype(jnp.bfloat16))
        coarse_kv.append(
            jnp.stack([current[1].astype(jnp.bfloat16), current[2].astype(jnp.bfloat16)])
        )
    fine_levels = [lev for lev in range(LEVELS) if tok_count >> lev >= BLOCK]
    far_levels = [lev for lev in range(LEVELS) if tok_count >> lev < BLOCK]
    rims = jnp.stack(
        [
            jnp.concatenate([coarse_kv[lev][:, :BLOCK], coarse_kv[lev][:, -BLOCK:]], axis=1)
            for lev in fine_levels
        ]
    )
    edged = with_halo(rims, (("seq", 2),), BLOCK)
    seg_wide = with_halo(segment, (("seq", 0),), BLOCK)
    results = []
    for slot_index, lev_index in enumerate(fine_levels):
        row_count = tok_count >> lev_index
        block_count = row_count // BLOCK
        widened = jnp.concatenate(
            [edged[slot_index, :, :BLOCK], coarse_kv[lev_index], edged[slot_index, :, 3 * BLOCK :]],
            axis=1,
        )
        pieces = widened.reshape(2, block_count + 2, BLOCK, head_count, HEAD_DIM)
        window = jnp.concatenate([pieces[:, :-2], pieces[:, 1:-1], pieces[:, 2:]], axis=2)
        neighbour = (
            seq_place * block_count + jnp.arange(block_count)[:, None] + jnp.arange(3)[None, :] - 1
        )
        usable = (neighbour >= 0) & (neighbour < seq_count * block_count)
        if lev_index > 0:
            usable = usable & (jnp.arange(3) != 1)[None, :]
        allowed = jnp.repeat(usable, BLOCK, axis=1)[:, None, :]
        if lev_index == 0:
            seg_pieces = seg_wide.reshape(block_count + 2, BLOCK)
            seg_window = jnp.concatenate(
                [seg_pieces[:-2], seg_pieces[1:-1], seg_pieces[2:]], axis=1
            )
            allowed = allowed & (
                segment.reshape(block_count, BLOCK)[:, :, None] == seg_window[:, None, :]
            )
        else:
            allowed = jnp.broadcast_to(allowed, (block_count, BLOCK, 3 * BLOCK))
        queries = coarse_q[lev_index].reshape(block_count, BLOCK, head_count, HEAD_DIM)
        peaks, totals, weighted = grouped_attend(queries, window[0], window[1], allowed, scaling)
        results.append(
            (
                lev_index,
                peaks.reshape(row_count, head_count),
                totals.reshape(row_count, head_count),
                weighted.reshape(row_count, head_count, HEAD_DIM),
            )
        )
    windows = {}
    for lev_index in far_levels:
        row_count = tok_count >> lev_index
        dev_span = BLOCK // row_count
        gathered = []
        for offset in range(-(2 * dev_span - 1), 2 * dev_span):
            if offset == 0:
                gathered.append(coarse_kv[lev_index])
            else:
                gathered.append(from_behind(coarse_kv[lev_index], "seq", -offset))
        beside_all = jnp.concatenate(gathered, axis=1)
        windows[lev_index] = lax.dynamic_slice_in_dim(
            beside_all, (dev_span - 1 - seq_place % dev_span) * row_count, 3 * BLOCK, 1
        )
    for lev_index in far_levels:
        row_count = tok_count >> lev_index
        dev_span = BLOCK // row_count
        own_block = seq_place // dev_span
        neighbour = own_block + jnp.arange(3) - 1
        usable = (neighbour >= 0) & (neighbour < seq_count // dev_span) & (jnp.arange(3) != 1)
        allowed = jnp.broadcast_to(
            jnp.repeat(usable, BLOCK)[None, None, :], (1, row_count, 3 * BLOCK)
        )
        window = windows[lev_index].reshape(2, 1, 3 * BLOCK, head_count, HEAD_DIM)
        queries = coarse_q[lev_index].reshape(1, row_count, head_count, HEAD_DIM)
        peaks, totals, weighted = block_attend(queries, window[0], window[1], allowed, scaling)
        results.append(
            (
                lev_index,
                peaks.reshape(row_count, head_count),
                totals.reshape(row_count, head_count),
                weighted.reshape(row_count, head_count, HEAD_DIM),
            )
        )
    run_peak = None
    run_total = None
    run_sum = None
    for lev_index, peaks, totals, weighted in results:
        factor = 2**lev_index
        peaks = jnp.repeat(peaks, factor, axis=0)
        totals = jnp.repeat(totals, factor, axis=0)
        weighted = jnp.repeat(weighted, factor, axis=0)
        if run_peak is None:
            run_peak, run_total, run_sum = (peaks, totals, weighted)
        else:
            new_peak = jnp.maximum(run_peak, peaks)
            old_scale = jnp.exp(run_peak - new_peak)
            new_scale = jnp.exp(peaks - new_peak)
            run_total = run_total * old_scale + totals * new_scale
            run_sum = run_sum * old_scale[..., None] + weighted * new_scale[..., None]
            run_peak = new_peak
    attention = (run_sum / run_total[..., None]).reshape(tok_count, feat_count).astype(jnp.bfloat16)
    projected = lax.psum_scatter(
        jnp.dot(attention, w_out, preferred_element_type=jnp.float32),
        "head",
        scatter_dimension=0,
        tiled=True,
    )
    return projected.astype(jnp.bfloat16)


def solution(mesh):
    placed = (P("seq", "head"), P("seq", "head"), P("seq", "head"), P("seq"), P("head", None))
    return jax.shard_map(
        on_device, mesh=mesh, in_specs=placed, out_specs=P(("seq", "head"), None), check_vma=False
    )
```

profile of v0, /device:TPU:1, one launch (start us, length us, event | category | flops | bytes accessed | tf_op | source)
XLA Modules:
  0.0 621.9 jit_solution(10123987630649471384)
XLA Ops:
  23.5 4.9 collective-permute-start
  75.8 9.1 %collective-permute-start.24 = (bf16[2,32,256]{2,1,0:T(8,128)(2,1)}, bf16[2,32,256]{2,1,0:T(8,128)(2,1)S(1)}, u32[]{:S(2)}, u32[]{:S(2)}) collective-permute-start(bf16[2,32,256]{2,1,0:T(8,128)(2,1)} %pad_maximum_fusion.9), channel_id=1, source_target_pairs={{0,60},{4,64},{8,68},{12,72},{16,76},{20,80},{24,84},{28,88},{32,9... | collective-permute-start | bytes 98312 | tf_op jit(solution)/shard_map/ppermute | solution.py:30
  92.1 6.2 %collective-permute-start.26 = (bf16[2,32,256]{2,1,0:T(8,128)(2,1)}, bf16[2,32,256]{2,1,0:T(8,128)(2,1)S(1)}, u32[]{:S(2)}, u32[]{:S(2)}) collective-permute-start(bf16[2,32,256]{2,1,0:T(8,128)(2,1)} %pad_maximum_fusion.9), channel_id=1, source_target_pairs={{0,52},{4,56},{8,60},{12,64},{16,68},{20,72},{24,76},{28,80},{32,8... | collective-permute-start | bytes 98312 | tf_op jit(solution)/shard_map/ppermute | solution.py:30
  99.6 5.5 collective-permute-start.27
  106.5 8.8 %collective-permute-start.28 = (bf16[2,32,256]{2,1,0:T(8,128)(2,1)}, bf16[2,32,256]{2,1,0:T(8,128)(2,1)S(1)}, u32[]{:S(2)}, u32[]{:S(2)}) collective-permute-start(bf16[2,32,256]{2,1,0:T(8,128)(2,1)} %pad_maximum_fusion.9), channel_id=1, source_target_pairs={{0,44},{4,48},{8,52},{12,56},{16,60},{20,64},{24,68},{28,72},{32,7... | collective-permute-start | bytes 98312 | tf_op jit(solution)/shard_map/ppermute | solution.py:30
  116.6 8.3 %collective-permute-start.29 = (bf16[2,32,256]{2,1,0:T(8,128)(2,1)}, bf16[2,32,256]{2,1,0:T(8,128)(2,1)S(1)}, u32[]{:S(2)}, u32[]{:S(2)}) collective-permute-start(bf16[2,32,256]{2,1,0:T(8,128)(2,1)} %pad_maximum_fusion.9), channel_id=1, source_target_pairs={{0,40},{4,44},{8,48},{12,52},{16,56},{20,60},{24,64},{28,68},{32,7... | collective-permute-start | bytes 98312 | tf_op jit(solution)/shard_map/ppermute | solution.py:30
  126.3 7.0 %collective-permute-start.30 = (bf16[2,32,256]{2,1,0:T(8,128)(2,1)}, bf16[2,32,256]{2,1,0:T(8,128)(2,1)S(1)}, u32[]{:S(2)}, u32[]{:S(2)}) collective-permute-start(bf16[2,32,256]{2,1,0:T(8,128)(2,1)} %pad_maximum_fusion.9), channel_id=1, source_target_pairs={{0,36},{4,40},{8,44},{12,48},{16,52},{20,56},{24,60},{28,64},{32,6... | collective-permute-start | bytes 98312 | tf_op jit(solution)/shard_map/ppermute | solution.py:30
  134.6 5.4 collective-permute-start.31
  141.3 8.4 %collective-permute-start.32 = (bf16[2,32,256]{2,1,0:T(8,128)(2,1)}, bf16[2,32,256]{2,1,0:T(8,128)(2,1)S(1)}, u32[]{:S(2)}, u32[]{:S(2)}) collective-permute-start(bf16[2,32,256]{2,1,0:T(8,128)(2,1)} %pad_maximum_fusion.9), channel_id=1, source_target_pairs={{0,28},{4,32},{8,36},{12,40},{16,44},{20,48},{24,52},{28,56},{32,6... | collective-permute-start | bytes 98312 | tf_op jit(solution)/shard_map/ppermute | solution.py:30
  151.0 9.6 %collective-permute-start.33 = (bf16[2,32,256]{2,1,0:T(8,128)(2,1)}, bf16[2,32,256]{2,1,0:T(8,128)(2,1)S(1)}, u32[]{:S(2)}, u32[]{:S(2)}) collective-permute-start(bf16[2,32,256]{2,1,0:T(8,128)(2,1)} %pad_maximum_fusion.9), channel_id=1, source_target_pairs={{0,24},{4,28},{8,32},{12,36},{16,40},{20,44},{24,48},{28,52},{32,5... | collective-permute-start | bytes 98312 | tf_op jit(solution)/shard_map/ppermute | solution.py:30
  162.0 6.6 %collective-permute-start.34 = (bf16[2,32,256]{2,1,0:T(8,128)(2,1)}, bf16[2,32,256]{2,1,0:T(8,128)(2,1)S(1)}, u32[]{:S(2)}, u32[]{:S(2)}) collective-permute-start(bf16[2,32,256]{2,1,0:T(8,128)(2,1)} %pad_maximum_fusion.9), channel_id=1, source_target_pairs={{0,20},{4,24},{8,28},{12,32},{16,36},{20,40},{24,44},{28,48},{32,5... | collective-permute-start | bytes 98312 | tf_op jit(solution)/shard_map/ppermute | solution.py:30
  169.9 6.0 collective-permute-start.35
  177.2 6.7 %collective-permute-start.36 = (bf16[2,32,256]{2,1,0:T(8,128)(2,1)}, bf16[2,32,256]{2,1,0:T(8,128)(2,1)S(1)}, u32[]{:S(2)}, u32[]{:S(2)}) collective-permute-start(bf16[2,32,256]{2,1,0:T(8,128)(2,1)} %pad_maximum_fusion.9), channel_id=1, source_target_pairs={{0,12},{4,16},{8,20},{12,24},{16,28},{20,32},{24,36},{28,40},{32,4... | collective-permute-start | bytes 98312 | tf_op jit(solution)/shard_map/ppermute | solution.py:30
  208.5 7.0 %collective-permute-done.41 = bf16[2,32,256]{2,1,0:T(8,128)(2,1)S(1)} collective-permute-done((bf16[2,32,256]{2,1,0:T(8,128)(2,1)}, bf16[2,32,256]{2,1,0:T(8,128)(2,1)S(1)}, u32[]{:S(2)}, u32[]{:S(2)}) %collective-permute-start.41) | collective-permute-done | bytes 32800 | tf_op jit(solution)/shard_map/ppermute | solution.py:30
  216.8 9.3 %collective-permute-done.42 = bf16[2,32,256]{2,1,0:T(8,128)(2,1)S(1)} collective-permute-done((bf16[2,32,256]{2,1,0:T(8,128)(2,1)}, bf16[2,32,256]{2,1,0:T(8,128)(2,1)S(1)}, u32[]{:S(2)}, u32[]{:S(2)}) %collective-permute-start.42) | collective-permute-done | bytes 32800 | tf_op jit(solution)/shard_map/ppermute | solution.py:30
  227.5 11.7 %collective-permute-done.43 = bf16[2,32,256]{2,1,0:T(8,128)(2,1)S(1)} collective-permute-done((bf16[2,32,256]{2,1,0:T(8,128)(2,1)}, bf16[2,32,256]{2,1,0:T(8,128)(2,1)S(1)}, u32[]{:S(2)}, u32[]{:S(2)}) %collective-permute-start.43) | collective-permute-done | bytes 32800 | tf_op jit(solution)/shard_map/ppermute | solution.py:30
  240.5 9.9 %collective-permute-done.44 = bf16[2,32,256]{2,1,0:T(8,128)(2,1)S(1)} collective-permute-done((bf16[2,32,256]{2,1,0:T(8,128)(2,1)}, bf16[2,32,256]{2,1,0:T(8,128)(2,1)S(1)}, u32[]{:S(2)}, u32[]{:S(2)}) %collective-permute-start.44) | collective-permute-done | bytes 32800 | tf_op jit(solution)/shard_map/ppermute | solution.py:30
  251.7 8.7 %collective-permute-done.45 = bf16[2,32,256]{2,1,0:T(8,128)(2,1)S(1)} collective-permute-done((bf16[2,32,256]{2,1,0:T(8,128)(2,1)}, bf16[2,32,256]{2,1,0:T(8,128)(2,1)S(1)}, u32[]{:S(2)}, u32[]{:S(2)}) %collective-permute-start.45) | collective-permute-done | bytes 32800 | tf_op jit(solution)/shard_map/ppermute | solution.py:30
  261.8 10.9 %collective-permute-done.46 = bf16[2,32,256]{2,1,0:T(8,128)(2,1)S(1)} collective-permute-done((bf16[2,32,256]{2,1,0:T(8,128)(2,1)}, bf16[2,32,256]{2,1,0:T(8,128)(2,1)S(1)}, u32[]{:S(2)}, u32[]{:S(2)}) %collective-permute-start.46) | collective-permute-done | bytes 32800 | tf_op jit(solution)/shard_map/ppermute | solution.py:30
  274.0 9.5 %collective-permute-done.47 = bf16[2,32,256]{2,1,0:T(8,128)(2,1)S(1)} collective-permute-done((bf16[2,32,256]{2,1,0:T(8,128)(2,1)}, bf16[2,32,256]{2,1,0:T(8,128)(2,1)S(1)}, u32[]{:S(2)}, u32[]{:S(2)}) %collective-permute-start.47) | collective-permute-done | bytes 32800 | tf_op jit(solution)/shard_map/ppermute | solution.py:30
  284.8 8.2 %collective-permute-done.48 = bf16[2,32,256]{2,1,0:T(8,128)(2,1)S(1)} collective-permute-done((bf16[2,32,256]{2,1,0:T(8,128)(2,1)}, bf16[2,32,256]{2,1,0:T(8,128)(2,1)S(1)}, u32[]{:S(2)}, u32[]{:S(2)}) %collective-permute-start.48) | collective-permute-done | bytes 32800 | tf_op jit(solution)/shard_map/ppermute | solution.py:30
  294.3 10.0 %collective-permute-done.49 = bf16[2,32,256]{2,1,0:T(8,128)(2,1)S(1)} collective-permute-done((bf16[2,32,256]{2,1,0:T(8,128)(2,1)}, bf16[2,32,256]{2,1,0:T(8,128)(2,1)S(1)}, u32[]{:S(2)}, u32[]{:S(2)}) %collective-permute-start.49) | collective-permute-done | bytes 32800 | tf_op jit(solution)/shard_map/ppermute | solution.py:30
  311.1 10.7 %collective-permute-start.10 = (bf16[2,64,256]{2,1,0:T(8,128)(2,1)}, bf16[2,64,256]{2,1,0:T(8,128)(2,1)}, u32[]{:S(2)}, u32[]{:S(2)}) collective-permute-start(bf16[2,64,256]{2,1,0:T(8,128)(2,1)} %pad_maximum_fusion.8), channel_id=1, source_target_pairs={{0,28},{4,32},{8,36},{12,40},{16,44},{20,48},{24,52},{28,56},{32,6... | collective-permute-start | bytes 196616 | tf_op jit(solution)/shard_map/ppermute | solution.py:30
  330.4 4.8 collective-permute-start.11
  337.1 9.5 %collective-permute-start.12 = (bf16[2,64,256]{2,1,0:T(8,128)(2,1)}, bf16[2,64,256]{2,1,0:T(8,128)(2,1)S(1)}, u32[]{:S(2)}, u32[]{:S(2)}) collective-permute-start(bf16[2,64,256]{2,1,0:T(8,128)(2,1)} %pad_maximum_fusion.8), channel_id=1, source_target_pairs={{0,20},{4,24},{8,28},{12,32},{16,36},{20,40},{24,44},{28,48},{32,5... | collective-permute-start | bytes 196616 | tf_op jit(solution)/shard_map/ppermute | solution.py:30
  348.7 5.2 collective-permute-start.13
  356.2 6.1 collective-permute-start.14
  389.9 6.6 %collective-permute-done.19 = bf16[2,64,256]{2,1,0:T(8,128)(2,1)S(1)} collective-permute-done((bf16[2,64,256]{2,1,0:T(8,128)(2,1)}, bf16[2,64,256]{2,1,0:T(8,128)(2,1)S(1)}, u32[]{:S(2)}, u32[]{:S(2)}) %collective-permute-start.19) | collective-permute-done | bytes 65568 | tf_op jit(solution)/shard_map/ppermute | solution.py:30
  402.8 9.5 %collective-permute-start.4 = (bf16[2,128,256]{2,1,0:T(8,128)(2,1)S(1)}, bf16[2,128,256]{2,1,0:T(8,128)(2,1)S(1)}, u32[]{:S(2)}, u32[]{:S(2)}) collective-permute-start(bf16[2,128,256]{2,1,0:T(8,128)(2,1)S(1)} %copy-done.41), channel_id=1, source_target_pairs={{0,12},{4,16},{8,20},{12,24},{16,28},{20,32},{24,36},{28,40},{32,4... | collective-permute-start | bytes 393224 | tf_op jit(solution)/shard_map/ppermute | solution.py:30
  496.6 5.0 pad_maximum_fusion
  504.4 16.0 %while.14 = (s32[]{:T(128)}, f32[2,2,256,4]{2,3,1,0:T(4,128)S(1)}, f32[2,2,256,4]{2,3,1,0:T(4,128)}, f32[2,2,256,4,64]{2,1,0,4,3:T(2,128)}, pred[2,2,256,768]{3,...) while((s32[]{:T(128)}, f32[2,2,256,4]{2,3,1,0:T(4,128)S(1)}, ...), condition=%wide.region_7.0_spmd, body=%wide.region_4.7_spmd.sunk | while | flops 423096320 | bytes 38995144 | solution.py:67
  547.4 65.1 %reduce-scatter.2.cloned.1.call-done = f32[256,1024]{1,0:T(8,128)} async-done(((f32[1024,1024]{1,0:T(8,128)}), f32[256,1024]{1,0:T(8,128)}) %reduce-scatter.2.cloned.1.call-update) | async-done | bytes 1048592 | tf_op jit(solution)/shard_map/reduce_scatter | solution.py:193
  (467 shorter events, 305.2 us)
Async XLA Ops:
  6.5 606.0 %reduce-scatter.2.cloned.1.call-start = ((), (), s32[]{:S(2)}) async-start(), calls=%async_computation.1 | async-start | bytes 5242880 | tf_op jit(solution)/shard_map/reduce_scatter | solution.py:193
  18.3 292.8 %collective-permute-start.53 = (bf16[2,32,256]{2,1,0:T(8,128)(2,1)}, bf16[2,32,256]{2,1,0:T(8,128)(2,1)}, u32[]{:S(2)}, u32[]{:S(2)}) collective-permute-start(bf16[2,32,256]{2,1,0:T(8,128)(2,1)} %pad_maximum_fusion.9), channel_id=1, source_target_pairs={{60,0},{64,4},{68,8},{72,12},{76,16},{80,20},{84,24},{88,28},{92,3... | collective-permute-start | bytes 98312 | tf_op jit(solution)/shard_map/ppermute | solution.py:30
  19.5 289.5 %collective-permute-start.52 = (bf16[2,32,256]{2,1,0:T(8,128)(2,1)}, bf16[2,32,256]{2,1,0:T(8,128)(2,1)}, u32[]{:S(2)}, u32[]{:S(2)}) collective-permute-start(bf16[2,32,256]{2,1,0:T(8,128)(2,1)} %pad_maximum_fusion.9), channel_id=1, source_target_pairs={{56,0},{60,4},{64,8},{68,12},{72,16},{76,20},{80,24},{84,28},{88,3... | collective-permute-start | bytes 98312 | tf_op jit(solution)/shard_map/ppermute | solution.py:30
  20.8 286.1 %collective-permute-start.51 = (bf16[2,32,256]{2,1,0:T(8,128)(2,1)}, bf16[2,32,256]{2,1,0:T(8,128)(2,1)}, u32[]{:S(2)}, u32[]{:S(2)}) collective-permute-start(bf16[2,32,256]{2,1,0:T(8,128)(2,1)} %pad_maximum_fusion.9), channel_id=1, source_target_pairs={{52,0},{56,4},{60,8},{64,12},{68,16},{72,20},{76,24},{80,28},{84,3... | collective-permute-start | bytes 98312 | tf_op jit(solution)/shard_map/ppermute | solution.py:30
  23.5 51.0 %collective-permute-start = (s32[256]{0:T(256)}, s32[256]{0:T(256)}, u32[]{:S(2)}, u32[]{:S(2)}) collective-permute-start(s32[256]{0:T(256)} %get-tuple-element.168), channel_id=1, source_target_pairs={{0,4},{4,8},{8,12},{12,16},{16,20},{20,24},{24,28},{28,32},{32,36}... | collective-permute-start | bytes 3080 | tf_op jit(solution)/shard_map/ppermute | solution.py:21
  28.4 47.4 %collective-permute-start.1 = (s32[256]{0:T(256)}, s32[256]{0:T(256)}, u32[]{:S(2)}, u32[]{:S(2)}) collective-permute-start(s32[256]{0:T(256)} %get-tuple-element.169), channel_id=1, source_target_pairs={{4,0},{8,4},{12,8},{16,12},{20,16},{24,20},{28,24},{32,28},{36,32}... | collective-permute-start | bytes 3080 | tf_op jit(solution)/shard_map/ppermute | solution.py:22
  74.5 231.1 %collective-permute-start.50 = (bf16[2,32,256]{2,1,0:T(8,128)(2,1)}, bf16[2,32,256]{2,1,0:T(8,128)(2,1)S(1)}, u32[]{:S(2)}, u32[]{:S(2)}) collective-permute-start(bf16[2,32,256]{2,1,0:T(8,128)(2,1)} %pad_maximum_fusion.9), channel_id=1, source_target_pairs={{48,0},{52,4},{56,8},{60,12},{64,16},{68,20},{72,24},{76,28},{80,3... | collective-permute-start | bytes 98312 | tf_op jit(solution)/shard_map/ppermute | solution.py:30
  75.8 10.5 %collective-permute-start.24 = (bf16[2,32,256]{2,1,0:T(8,128)(2,1)}, bf16[2,32,256]{2,1,0:T(8,128)(2,1)S(1)}, u32[]{:S(2)}, u32[]{:S(2)}) collective-permute-start(bf16[2,32,256]{2,1,0:T(8,128)(2,1)} %pad_maximum_fusion.9), channel_id=1, source_target_pairs={{0,60},{4,64},{8,68},{12,72},{16,76},{20,80},{24,84},{28,88},{32,9... | collective-permute-start | bytes 98312 | tf_op jit(solution)/shard_map/ppermute | solution.py:30
  106.5 10.1 %collective-permute-start.28 = (bf16[2,32,256]{2,1,0:T(8,128)(2,1)}, bf16[2,32,256]{2,1,0:T(8,128)(2,1)S(1)}, u32[]{:S(2)}, u32[]{:S(2)}) collective-permute-start(bf16[2,32,256]{2,1,0:T(8,128)(2,1)} %pad_maximum_fusion.9), channel_id=1, source_target_pairs={{0,44},{4,48},{8,52},{12,56},{16,60},{20,64},{24,68},{28,72},{32,7... | collective-permute-start | bytes 98312 | tf_op jit(solution)/shard_map/ppermute | solution.py:30
  116.6 9.7 %collective-permute-start.29 = (bf16[2,32,256]{2,1,0:T(8,128)(2,1)}, bf16[2,32,256]{2,1,0:T(8,128)(2,1)S(1)}, u32[]{:S(2)}, u32[]{:S(2)}) collective-permute-start(bf16[2,32,256]{2,1,0:T(8,128)(2,1)} %pad_maximum_fusion.9), channel_id=1, source_target_pairs={{0,40},{4,44},{8,48},{12,52},{16,56},{20,60},{24,64},{28,68},{32,7... | collective-permute-start | bytes 98312 | tf_op jit(solution)/shard_map/ppermute | solution.py:30
  141.3 9.7 %collective-permute-start.32 = (bf16[2,32,256]{2,1,0:T(8,128)(2,1)}, bf16[2,32,256]{2,1,0:T(8,128)(2,1)S(1)}, u32[]{:S(2)}, u32[]{:S(2)}) collective-permute-start(bf16[2,32,256]{2,1,0:T(8,128)(2,1)} %pad_maximum_fusion.9), channel_id=1, source_target_pairs={{0,28},{4,32},{8,36},{12,40},{16,44},{20,48},{24,52},{28,56},{32,6... | collective-permute-start | bytes 98312 | tf_op jit(solution)/shard_map/ppermute | solution.py:30
  151.0 10.9 %collective-permute-start.33 = (bf16[2,32,256]{2,1,0:T(8,128)(2,1)}, bf16[2,32,256]{2,1,0:T(8,128)(2,1)S(1)}, u32[]{:S(2)}, u32[]{:S(2)}) collective-permute-start(bf16[2,32,256]{2,1,0:T(8,128)(2,1)} %pad_maximum_fusion.9), channel_id=1, source_target_pairs={{0,24},{4,28},{8,32},{12,36},{16,40},{20,44},{24,48},{28,52},{32,5... | collective-permute-start | bytes 98312 | tf_op jit(solution)/shard_map/ppermute | solution.py:30
  215.5 10.7 %collective-permute-start.42 = (bf16[2,32,256]{2,1,0:T(8,128)(2,1)}, bf16[2,32,256]{2,1,0:T(8,128)(2,1)S(1)}, u32[]{:S(2)}, u32[]{:S(2)}) collective-permute-start(bf16[2,32,256]{2,1,0:T(8,128)(2,1)} %pad_maximum_fusion.9), channel_id=1, source_target_pairs={{16,0},{20,4},{24,8},{28,12},{32,16},{36,20},{40,24},{44,28},{48,3... | collective-permute-start | bytes 98312 | tf_op jit(solution)/shard_map/ppermute | solution.py:30
  226.2 13.0 %collective-permute-start.43 = (bf16[2,32,256]{2,1,0:T(8,128)(2,1)}, bf16[2,32,256]{2,1,0:T(8,128)(2,1)S(1)}, u32[]{:S(2)}, u32[]{:S(2)}) collective-permute-start(bf16[2,32,256]{2,1,0:T(8,128)(2,1)} %pad_maximum_fusion.9), channel_id=1, source_target_pairs={{20,0},{24,4},{28,8},{32,12},{36,16},{40,20},{44,24},{48,28},{52,3... | collective-permute-start | bytes 98312 | tf_op jit(solution)/shard_map/ppermute | solution.py:30
  239.2 11.2 %collective-permute-start.44 = (bf16[2,32,256]{2,1,0:T(8,128)(2,1)}, bf16[2,32,256]{2,1,0:T(8,128)(2,1)S(1)}, u32[]{:S(2)}, u32[]{:S(2)}) collective-permute-start(bf16[2,32,256]{2,1,0:T(8,128)(2,1)} %pad_maximum_fusion.9), channel_id=1, source_target_pairs={{24,0},{28,4},{32,8},{36,12},{40,16},{44,20},{48,24},{52,28},{56,3... | collective-permute-start | bytes 98312 | tf_op jit(solution)/shard_map/ppermute | solution.py:30
  250.4 10.0 %collective-permute-start.45 = (bf16[2,32,256]{2,1,0:T(8,128)(2,1)}, bf16[2,32,256]{2,1,0:T(8,128)(2,1)S(1)}, u32[]{:S(2)}, u32[]{:S(2)}) collective-permute-start(bf16[2,32,256]{2,1,0:T(8,128)(2,1)} %pad_maximum_fusion.9), channel_id=1, source_target_pairs={{28,0},{32,4},{36,8},{40,12},{44,16},{48,20},{52,24},{56,28},{60,3... | collective-permute-start | bytes 98312 | tf_op jit(solution)/shard_map/ppermute | solution.py:30
  260.5 12.2 %collective-permute-start.46 = (bf16[2,32,256]{2,1,0:T(8,128)(2,1)}, bf16[2,32,256]{2,1,0:T(8,128)(2,1)S(1)}, u32[]{:S(2)}, u32[]{:S(2)}) collective-permute-start(bf16[2,32,256]{2,1,0:T(8,128)(2,1)} %pad_maximum_fusion.9), channel_id=1, source_target_pairs={{32,0},{36,4},{40,8},{44,12},{48,16},{52,20},{56,24},{60,28},{64,3... | collective-permute-start | bytes 98312 | tf_op jit(solution)/shard_map/ppermute | solution.py:30
  272.7 10.8 %collective-permute-start.47 = (bf16[2,32,256]{2,1,0:T(8,128)(2,1)}, bf16[2,32,256]{2,1,0:T(8,128)(2,1)S(1)}, u32[]{:S(2)}, u32[]{:S(2)}) collective-permute-start(bf16[2,32,256]{2,1,0:T(8,128)(2,1)} %pad_maximum_fusion.9), channel_id=1, source_target_pairs={{36,0},{40,4},{44,8},{48,12},{52,16},{56,20},{60,24},{64,28},{68,3... | collective-permute-start | bytes 98312 | tf_op jit(solution)/shard_map/ppermute | solution.py:30
  293.0 11.3 %collective-permute-start.49 = (bf16[2,32,256]{2,1,0:T(8,128)(2,1)}, bf16[2,32,256]{2,1,0:T(8,128)(2,1)S(1)}, u32[]{:S(2)}, u32[]{:S(2)}) collective-permute-start(bf16[2,32,256]{2,1,0:T(8,128)(2,1)} %pad_maximum_fusion.9), channel_id=1, source_target_pairs={{44,0},{48,4},{52,8},{56,12},{60,16},{64,20},{68,24},{72,28},{76,3... | collective-permute-start | bytes 98312 | tf_op jit(solution)/shard_map/ppermute | solution.py:30
  304.3 108.8 %collective-permute-start.23 = (bf16[2,64,256]{2,1,0:T(8,128)(2,1)}, bf16[2,64,256]{2,1,0:T(8,128)(2,1)}, u32[]{:S(2)}, u32[]{:S(2)}) collective-permute-start(bf16[2,64,256]{2,1,0:T(8,128)(2,1)} %pad_maximum_fusion.8), channel_id=1, source_target_pairs={{28,0},{32,4},{36,8},{40,12},{44,16},{48,20},{52,24},{56,28},{60,3... | collective-permute-start | bytes 196616 | tf_op jit(solution)/shard_map/ppermute | solution.py:30
  305.6 97.1 %collective-permute-start.22 = (bf16[2,64,256]{2,1,0:T(8,128)(2,1)}, bf16[2,64,256]{2,1,0:T(8,128)(2,1)}, u32[]{:S(2)}, u32[]{:S(2)}) collective-permute-start(bf16[2,64,256]{2,1,0:T(8,128)(2,1)} %pad_maximum_fusion.8), channel_id=1, source_target_pairs={{24,0},{28,4},{32,8},{36,12},{40,16},{44,20},{48,24},{52,28},{56,3... | collective-permute-start | bytes 196616 | tf_op jit(solution)/shard_map/ppermute | solution.py:30
  307.0 93.1 %collective-permute-start.21 = (bf16[2,64,256]{2,1,0:T(8,128)(2,1)}, bf16[2,64,256]{2,1,0:T(8,128)(2,1)}, u32[]{:S(2)}, u32[]{:S(2)}) collective-permute-start(bf16[2,64,256]{2,1,0:T(8,128)(2,1)} %pad_maximum_fusion.8), channel_id=1, source_target_pairs={{20,0},{24,4},{28,8},{32,12},{36,16},{40,20},{44,24},{48,28},{52,3... | collective-permute-start | bytes 196616 | tf_op jit(solution)/shard_map/ppermute | solution.py:30
  309.0 88.8 %collective-permute-start.20 = (bf16[2,64,256]{2,1,0:T(8,128)(2,1)}, bf16[2,64,256]{2,1,0:T(8,128)(2,1)}, u32[]{:S(2)}, u32[]{:S(2)}) collective-permute-start(bf16[2,64,256]{2,1,0:T(8,128)(2,1)} %pad_maximum_fusion.8), channel_id=1, source_target_pairs={{16,0},{20,4},{24,8},{28,12},{32,16},{36,20},{40,24},{44,28},{48,3... | collective-permute-start | bytes 196616 | tf_op jit(solution)/shard_map/ppermute | solution.py:30
  311.1 19.3 %collective-permute-start.10 = (bf16[2,64,256]{2,1,0:T(8,128)(2,1)}, bf16[2,64,256]{2,1,0:T(8,128)(2,1)}, u32[]{:S(2)}, u32[]{:S(2)}) collective-permute-start(bf16[2,64,256]{2,1,0:T(8,128)(2,1)} %pad_maximum_fusion.8), channel_id=1, source_target_pairs={{0,28},{4,32},{8,36},{12,40},{16,44},{20,48},{24,52},{28,56},{32,6... | collective-permute-start | bytes 196616 | tf_op jit(solution)/shard_map/ppermute | solution.py:30
  337.1 11.6 %collective-permute-start.12 = (bf16[2,64,256]{2,1,0:T(8,128)(2,1)}, bf16[2,64,256]{2,1,0:T(8,128)(2,1)S(1)}, u32[]{:S(2)}, u32[]{:S(2)}) collective-permute-start(bf16[2,64,256]{2,1,0:T(8,128)(2,1)} %pad_maximum_fusion.8), channel_id=1, source_target_pairs={{0,20},{4,24},{8,28},{12,32},{16,36},{20,40},{24,44},{28,48},{32,5... | collective-permute-start | bytes 196616 | tf_op jit(solution)/shard_map/ppermute | solution.py:30
  396.6 32.9 %collective-permute-start.9 = (bf16[2,128,256]{2,1,0:T(8,128)(2,1)S(1)}, bf16[2,128,256]{2,1,0:T(8,128)(2,1)S(1)}, u32[]{:S(2)}, u32[]{:S(2)}) collective-permute-start(bf16[2,128,256]{2,1,0:T(8,128)(2,1)S(1)} %copy-done.41), channel_id=1, source_target_pairs={{12,0},{16,4},{20,8},{24,12},{28,16},{32,20},{36,24},{40,28},{44,3... | collective-permute-start | bytes 393224 | tf_op jit(solution)/shard_map/ppermute | solution.py:30
  397.9 31.6 %collective-permute-start.8 = (bf16[2,128,256]{2,1,0:T(8,128)(2,1)S(1)}, bf16[2,128,256]{2,1,0:T(8,128)(2,1)S(1)}, u32[]{:S(2)}, u32[]{:S(2)}) collective-permute-start(bf16[2,128,256]{2,1,0:T(8,128)(2,1)S(1)} %copy-done.41), channel_id=1, source_target_pairs={{8,0},{12,4},{16,8},{20,12},{24,16},{28,20},{32,24},{36,28},{40,32... | collective-permute-start | bytes 393224 | tf_op jit(solution)/shard_map/ppermute | solution.py:30
  400.0 29.4 %collective-permute-start.7 = (bf16[2,128,256]{2,1,0:T(8,128)(2,1)S(1)}, bf16[2,128,256]{2,1,0:T(8,128)(2,1)S(1)}, u32[]{:S(2)}, u32[]{:S(2)}) collective-permute-start(bf16[2,128,256]{2,1,0:T(8,128)(2,1)S(1)} %copy-done.41), channel_id=1, source_target_pairs={{4,0},{8,4},{12,8},{16,12},{20,16},{24,20},{28,24},{32,28},{36,32}... | collective-permute-start | bytes 393224 | tf_op jit(solution)/shard_map/ppermute | solution.py:30
  402.8 15.8 %collective-permute-start.4 = (bf16[2,128,256]{2,1,0:T(8,128)(2,1)S(1)}, bf16[2,128,256]{2,1,0:T(8,128)(2,1)S(1)}, u32[]{:S(2)}, u32[]{:S(2)}) collective-permute-start(bf16[2,128,256]{2,1,0:T(8,128)(2,1)S(1)} %copy-done.41), channel_id=1, source_target_pairs={{0,12},{4,16},{8,20},{12,24},{16,28},{20,32},{24,36},{28,40},{32,4... | collective-permute-start | bytes 393224 | tf_op jit(solution)/shard_map/ppermute | solution.py:30
  413.2 9.8 %collective-permute-start.5 = (bf16[2,128,256]{2,1,0:T(8,128)(2,1)S(1)}, bf16[2,128,256]{2,1,0:T(8,128)(2,1)S(1)}, u32[]{:S(2)}, u32[]{:S(2)}) collective-permute-start(bf16[2,128,256]{2,1,0:T(8,128)(2,1)S(1)} %copy-done.41), channel_id=1, source_target_pairs={{0,8},{4,12},{8,16},{12,20},{16,24},{20,28},{24,32},{28,36},{32,40... | collective-permute-start | bytes 393224 | tf_op jit(solution)/shard_map/ppermute | solution.py:30
  423.0 32.5 %collective-permute-start.2 = (bf16[3,2,256,256]{3,2,1,0:T(8,128)(2,1)}, bf16[3,2,256,256]{3,2,1,0:T(8,128)(2,1)}, u32[]{:S(2)}, u32[]{:S(2)}) collective-permute-start(bf16[3,2,256,256]{3,2,1,0:T(8,128)(2,1)} %get-tuple-element.128), channel_id=1, source_target_pairs={{0,4},{4,8},{8,12},{12,16},{16,20},{20,24},{24,28},{28,32},{32,36}... | collective-permute-start | bytes 2359304 | tf_op jit(solution)/shard_map/ppermute | solution.py:21
  427.4 30.1 %collective-permute-start.3 = (bf16[3,2,256,256]{3,2,1,0:T(8,128)(2,1)}, bf16[3,2,256,256]{3,2,1,0:T(8,128)(2,1)}, u32[]{:S(2)}, u32[]{:S(2)}) collective-permute-start(bf16[3,2,256,256]{3,2,1,0:T(8,128)(2,1)} %get-tuple-element.129), channel_id=1, source_target_pairs={{4,0},{8,4},{12,8},{16,12},{20,16},{24,20},{28,24},{32,28},{36,32}... | collective-permute-start | bytes 2359304 | tf_op jit(solution)/shard_map/ppermute | solution.py:22
  (93 other events, 1938.6 us)
Sparse Core Ops, SparseCore 0:
  547.5 64.9 reduce-scatter.1
where the time goes:
time: 632 us; the launch traced here: 622 us
  starting transfers between devices  211 us (33%)
  waiting for transfers between devices  202 us (32%)
  local copies, waits for them, and re-layouts  115 us (18%)
  other arithmetic  56.9 us (9%)
  matrix products  20.3 us (3%)
  between operations  16 us (3%)
    ppermute x50, starting transfers between devices, from_behind(): return lax.ppermute(array, axis, pairs)  198 us
    ppermute x50, waiting for transfers between devices, from_behind(): return lax.ppermute(array, axis, pairs)  137 us
    reduce_scatter x1, waiting for transfers between devices, on_device(): lax.psum_scatter(jnp.dot(attention, w_out, preferred_element_type=jnp.flo...  65.1 us
    reshape x10, local copies, waits for them, and re-layouts, on_device(): weighted = jnp.repeat(weighted, factor, axis=0)  23.7 us
    reduce_sum x15, other arithmetic, on_device(): jnp.mean(source.reshape(half_rows, 2, feat_count), axis=1)  16.2 us
    unnamed x183, local copies, waits for them, and re-layouts  14.4 us
  transfers between devices with their start and end apart: 55, of which 35 were waited for; matrix products, arithmetic and copies ran while one was open for 14% of the time, Pallas kernels for 0%

commit v1 on v0

v1 whole, which is shorter than its diff:
```python
import jax
import jax.numpy as jnp
from jax import lax
from jax.experimental import pallas as pl
from jax.experimental.pallas import tpu as pltpu
from jax.sharding import PartitionSpec as P

MESH = pl.DeviceIdType.MESH
F32 = jnp.float32
BF16 = jnp.bfloat16

SEQ = 64
HEADX = 4
BLOCK = 256
ROWS = 1024
NEG = -1e30
BIG = 1e30

SEG_P, SEG_N, L0_P, L0_N, L1_P, L1_N, L2_P, L2_N = range(8)
KV3, KV4, KV5, Q3, RES3 = range(8, 13)
Q45, RES45, WG, WF, AT = 12, 15, 18, 21, 24
N_SEM = 28


def averaging():
    row = lax.broadcasted_iota(jnp.int32, (BLOCK, BLOCK), 0)
    token = lax.broadcasted_iota(jnp.int32, (BLOCK, BLOCK), 1)
    result = jnp.zeros((BLOCK, BLOCK), F32)
    base = 0
    for level in range(1, 6):
        count = BLOCK >> level
        first = (row - base) << level
        hit = (row >= base) & (row < base + count) & (token >= first) & (token < first + (1 << level))
        result = jnp.where(hit, 0.5**level, result)
        base += count
    return result.astype(BF16)


def scores_of(q, k):
    return lax.dot_general(q, k, (((1,), (1,)), ((), ())), preferred_element_type=F32)


def attend(q, keys, values, biases, present):
    scores = [scores_of(q, k) for k in keys]
    if biases is not None:
        scores = [s + b for s, b in zip(scores, biases)]
    tops = [jnp.max(s, axis=1, keepdims=True) for s in scores]
    if present is not None:
        tops = [jnp.where(ok, t, NEG) for ok, t in zip(present, tops)]
    peak = tops[0]
    for t in tops[1:]:
        peak = jnp.maximum(peak, t)
    total = None
    for index, (s, v) in enumerate(zip(scores, values)):
        shift = peak if present is None else jnp.where(present[index], peak, BIG)
        probs = jnp.exp(s - shift).astype(BF16)
        part = jnp.dot(probs, v, preferred_element_type=F32)
        total = part if total is None else total + part
    return total, peak


def pair(q, keys, values, biases, present, low_half, lo, hi):
    even, even_peak = attend(q * lo, keys, [v * lo + hi for v in values], biases, present)
    odd, odd_peak = attend(q * hi, keys, [v * hi + lo for v in values], biases, present)
    num = jnp.where(low_half, even, odd)
    total = pltpu.roll(jnp.where(low_half, odd, even), 64, 1)
    peak = jnp.where(low_half, even_peak, odd_peak)
    return num, total, peak


def merge(a, b):
    peak = jnp.maximum(a[2], b[2])
    scale_a, scale_b = jnp.exp(a[2] - peak), jnp.exp(b[2] - peak)
    return a[0] * scale_a + b[0] * scale_b, a[1] * scale_a + b[1] * scale_b, peak


def expand(parts, ref):
    count = parts[0].shape[0]
    for index, part in enumerate(parts):
        ref[index, pl.ds(0, count, stride=2), :] = part
        ref[index, pl.ds(1, count, stride=2), :] = part
    return tuple(ref[index, 0 : 2 * count, :] for index in range(3))


def kernel(
    q_hbm, k_hbm, v_hbm, seg_hbm, w_hbm, out_ref,
    q0, kv0, segi, segf, q1, kv1, q2, kv2,
    s3, r3, sq3, rq3, s4, r4, s5, r5, sq45, rq45,
    st0, st1, st2, st3, rs3, srow, rrow, ex, at, ra, wbuf,
    local, snd, rcv,
):
    i = lax.axis_index("seq")
    x = lax.axis_index("head")
    core = lax.rem(i, 2)
    chip = lax.div(i, 2)
    g4, a4 = lax.div(i, 4), lax.rem(i, 4)
    g5, a5 = lax.div(i, 8), lax.rem(i, 8)
    sibling = i + 1 - 2 * core
    right, left = lax.rem(i + 1, SEQ), lax.rem(i + SEQ - 1, SEQ)

    def remote(src, dst, slot, device):
        return pltpu.make_async_remote_copy(
            src_ref=src, dst_ref=dst, send_sem=snd.at[slot], recv_sem=rcv.at[slot], device_id=device, device_id_type=MESH
        )

    loads = []
    for p in range(2):
        lanes = pl.ds(128 * p, 128)
        loads.append(pltpu.make_async_copy(k_hbm.at[:, lanes], kv0.at[0, p, pl.ds(BLOCK, ROWS)], local.at[p]))
        loads.append(pltpu.make_async_copy(v_hbm.at[:, lanes], kv0.at[1, p, pl.ds(BLOCK, ROWS)], local.at[2 + p]))
        loads.append(pltpu.make_async_copy(q_hbm.at[:, lanes], q0.at[p], local.at[4 + p]))
    loads.append(pltpu.make_async_copy(seg_hbm, segi.at[1], local.at[6]))
    load_w = pltpu.make_async_copy(w_hbm, wbuf.at[x], local.at[7])
    for load in loads:
        load.start()
    load_w.start()

    barrier = pltpu.get_barrier_semaphore()

    def greet(seq, head):
        pl.semaphore_signal(barrier, inc=1, device_id={"seq": seq, "head": head}, device_id_type=MESH)

    blocks4 = [lax.rem(g4 + 1, SEQ // 4), lax.rem(g4 + SEQ // 4 - 1, SEQ // 4)]
    blocks5 = [lax.rem(g5 + 1, SEQ // 8), lax.rem(g5 + SEQ // 8 - 1, SEQ // 8)]
    for block in blocks5:
        for j in range(8):
            greet(block * 8 + j, x)
    for block in blocks4:
        for j in range(4):
            greet(block * 4 + j, x)
    for d in range(1, 4):
        greet(g4 * 4 + lax.rem(a4 + d, 4), x)
        greet(i, lax.rem(x + d, HEADX))

    lane = lax.broadcasted_iota(jnp.int32, (1, 128), 1)
    low_half = lane < 64
    lo_f = jnp.where(low_half, 1.0, 0.0).astype(F32)
    lo = lo_f.astype(BF16)
    hi = (1.0 - lo_f).astype(BF16)
    means = averaging()
    for load in loads:
        load.wait()
    last_k, last_v, last_q = [], [], []
    for t in range(4):
        rows = pl.ds(BLOCK + BLOCK * t, BLOCK)
        ck, cv = [
            jnp.dot(means, jnp.concatenate([kv0[n, 0, rows, :], kv0[n, 1, rows, :]], axis=1), preferred_element_type=F32)
            for n in range(2)
        ]
        own = pl.ds(BLOCK * t, BLOCK)
        cq = 0.125 * jnp.dot(means, jnp.concatenate([q0[0, own, :], q0[1, own, :]], axis=1), preferred_element_type=F32)
        for p in range(2):
            lanes = slice(128 * p, 128 * p + 128)
            q1[p, pl.ds(128 * t, 128), :] = cq[0:128, lanes].astype(BF16)
            q2[p, pl.ds(64 * t, 64), :] = cq[128:192, lanes].astype(BF16)
            sq3[p, pl.ds(32 * t, 32), :] = cq[192:224, lanes].astype(BF16)
            for n, c in enumerate((ck, cv)):
                kv1[n, p, pl.ds(BLOCK + 128 * t, 128), :] = c[0:128, lanes].astype(BF16)
                kv2[n, p, pl.ds(BLOCK + 64 * t, 64), :] = c[128:192, lanes].astype(BF16)
                s3[p, n, pl.ds(32 * t, 32), :] = c[192:224, lanes].astype(BF16)
        for h in range(4):
            s4[h, pl.ds(16 * t, 16), :] = packed(ck[224:240], cv[224:240], h, low_half).astype(BF16)
            sq45[h, pl.ds(16 * t, 16), :] = packed(cq[224:240], None, h, low_half).astype(BF16)
        last_k.append(ck[240:248])
        last_v.append(cv[240:248])
        last_q.append(cq[240:248])
    k5, v5, q5 = [jnp.concatenate(rows, axis=0) for rows in (last_k, last_v, last_q)]
    for h in range(4):
        s5[h] = packed(k5, v5, h, low_half).astype(BF16)
        sq45[h, pl.ds(64, 32), :] = packed(q5, None, h, low_half).astype(BF16)

    pl.semaphore_wait(barrier, 30)
    sends = []

    def send(src, dst, slot, seq, head=x):
        copy = remote(src, dst, slot, {"seq": seq, "head": head})
        copy.start()
        return copy

    half = pl.ds(128 * core, 128)
    for d in (1, 3, 2):
        sends.append(send(w_hbm.at[half], wbuf.at[x, half], WG + d, i, lax.rem(x + d, HEADX)))
    sends.append(send(sq3.at[1 - core], rq3.at[core], Q3, sibling))
    for d in range(1, 4):
        other = lax.rem(a4 + d, 4)
        sends.append(send(sq45.at[other], rq45.at[a4], Q45 + d, g4 * 4 + other))
    for direction, block in enumerate(blocks5):
        for j in range(8):
            send(s5.at[j % 4], r5.at[direction, a5], KV5, block * 8 + j)
    for direction, block in enumerate(blocks4):
        for j in range(4):
            send(s4.at[j], r4.at[direction, a4], KV4, block * 4 + j)
    for direction, by in enumerate((1, SEQ // 2 - 1)):
        beside = lax.rem(chip + by, SEQ // 2)
        for p in range(2):
            send(s3.at[p], r3.at[direction, :, core], KV3, beside * 2 + p)
    sends.append(send(segi.at[1], segi.at[0], SEG_P, right))
    sends.append(send(segi.at[1], segi.at[2], SEG_N, left))
    for ref, count, slot in ((kv2, 256, L2_P), (kv1, 512, L1_P), (kv0, 1024, L0_P)):
        sends.append(
            send(ref.at[:, :, pl.ds(count, BLOCK)], ref.at[:, :, pl.ds(0, BLOCK)], slot, right)
        )
        sends.append(
            send(ref.at[:, :, pl.ds(BLOCK, BLOCK)], ref.at[:, :, pl.ds(BLOCK + count, BLOCK)], slot + 1, left)
        )
    rq3[core] = sq3[core]
    rq45[a4] = sq45[a4]

    def received(ref, slot):
        pltpu.make_async_copy(ref, ref, rcv.at[slot]).wait()

    def sent(ref, slot):
        pltpu.make_async_copy(ref, ref, snd.at[slot]).wait()

    received(segi.at[0], SEG_P)
    received(segi.at[2], SEG_N)
    for n in range(3):
        segf[pl.ds(8 * n, 8), :] = segi[n].astype(F32)

    def bias_of(b, j):
        exists = (4 * i + b + j >= 1) & (4 * i + b + j <= 4 * SEQ)
        first = 6 + 2 * (b + j)
        return [jnp.where(exists, segf[pl.ds(first + n, 1), :], -1.0) for n in range(2)]

    def level0(b, p):
        queries = q0[p, pl.ds(pl.multiple_of(b * BLOCK, BLOCK), BLOCK), :] * jnp.asarray(0.125, BF16)
        own = [
            jnp.transpose(jnp.broadcast_to(segf[pl.ds(8 + 2 * b + n, 1), :], (128, 128))) for n in range(2)
        ]
        own = jnp.concatenate(own, axis=0)
        keys, values, biases = [], [], []
        for j in range(3):
            rows = pl.ds(pl.multiple_of((b + j) * BLOCK, BLOCK), BLOCK)
            keys.append(kv0[0, p, rows, :])
            values.append(kv0[1, p, rows, :])
            biases.append(
                jnp.concatenate([jnp.where(own == near, 0.0, NEG) for near in bias_of(b, j)], axis=1)
            )
        state = pair(queries, keys, values, biases, None, low_half, lo, hi)
        for n in range(3):
            st0[n, p, pl.ds(pl.multiple_of(b * BLOCK, BLOCK), BLOCK), :] = state[n]

    @pl.loop(0, 4)
    def _(u):
        level0(1 + lax.div(u, 2), lax.rem(u, 2))

    for d in (1, 3, 2):
        owner = lax.rem(x + HEADX - d, HEADX)
        received(wbuf.at[owner, half], WG + d)
        sends.append(send(wbuf.at[owner, half], wbuf.at[owner, half], WF + d, sibling))

    for d in range(1, 4):
        received(rq45.at[lax.rem(a4 + 4 - d, 4)], Q45 + d)

    def one_head(ref, queries, first, rows, place, count):
        block_rows = ref.shape[1] * ref.shape[2]
        tiles = [ref[n].reshape(block_rows, 128) for n in range(2)]
        out, peak = attend(queries, tiles, [t * hi + lo for t in tiles], None, (place > 0, place < count - 1))
        out = jnp.where((lane >= 32) & low_half, peak, out)
        for n in range(4):
            srow[n, pl.ds(first, rows), :] = out[n * rows : (n + 1) * rows]

    received(r5, KV5)
    one_head(r5, rq45[:, 64:96, :].reshape(128, 128), 64, 32, g5, SEQ // 8)
    received(r4, KV4)
    one_head(r4, rq45[:, 0:64, :].reshape(256, 128), 0, 64, g4, SEQ // 4)
    for d in range(1, 4):
        other = lax.rem(a4 + d, 4)
        sends.append(send(srow.at[other], rrow.at[a4], RES45 + d, g4 * 4 + other))
    rrow[a4] = srow[a4]

    received(r3, KV3)
    received(rq3.at[1 - core], Q3)
    state = pair(
        rq3[...].reshape(256, 128),
        [r3[n, 0].reshape(256, 128) for n in range(2)],
        [r3[n, 1].reshape(256, 128) for n in range(2)],
        None,
        (chip > 0, chip < SEQ // 2 - 1),
        low_half, lo, hi,
    )
    for n in range(3):
        for m in range(2):
            rs3[m, n] = state[n][128 * m : 128 * m + 128]
    sends.append(send(rs3.at[1 - core], st3.at[core], RES3, sibling))
    st3[core] = rs3[core]

    received(kv2.at[:, :, pl.ds(0, BLOCK)], L2_P)
    received(kv2.at[:, :, pl.ds(2 * BLOCK, BLOCK)], L2_N)

    @pl.loop(0, 2)
    def _(p):
        sides = [pl.ds(0, BLOCK), pl.ds(2 * BLOCK, BLOCK)]
        state = pair(
            q2[p], [kv2[0, p, s, :] for s in sides], [kv2[1, p, s, :] for s in sides],
            None, (i > 0, i < SEQ - 1), low_half, lo, hi,
        )
        for n in range(3):
            st2[n, p] = state[n]

    received(kv1.at[:, :, pl.ds(0, BLOCK)], L1_P)
    received(kv1.at[:, :, pl.ds(3 * BLOCK, BLOCK)], L1_N)

    @pl.loop(0, 4)
    def _(u):
        b, p = lax.div(u, 2), lax.rem(u, 2)
        own = pl.ds(pl.multiple_of(b * BLOCK, BLOCK), BLOCK)
        sides = [own, pl.ds(pl.multiple_of((b + 2) * BLOCK, BLOCK), BLOCK)]
        place = 2 * i + b
        state = pair(
            q1[p, own, :], [kv1[0, p, s, :] for s in sides], [kv1[1, p, s, :] for s in sides],
            None, (place > 0, place < 2 * SEQ - 1), low_half, lo, hi,
        )
        for n in range(3):
            st1[n, p, own, :] = state[n]

    for d in range(1, 4):
        received(rrow.at[lax.rem(a4 + 4 - d, 4)], RES45 + d)
    received(st3.at[1 - core], RES3)
    for p in range(2):

        def far(rows):
            even, odd = rrow[2 * p, rows, :], rrow[2 * p + 1, rows, :]
            num = jnp.where(low_half, pltpu.roll(even, 64, 1), odd)
            total = jnp.where(low_half, even[:, 0:1], odd[:, 0:1])
            return num, total, jnp.where(low_half, even[:, 32:33], odd[:, 32:33])

        state = merge(expand(far(slice(64, 96)), ex), far(slice(0, 64)))
        state = merge(expand(state, ex), tuple(st3[p, n] for n in range(3)))
        state = merge(expand(state, ex), tuple(st2[n, p] for n in range(3)))
        state = merge(expand(state, ex), tuple(st1[n, p] for n in range(3)))
        for n in range(3):
            st1[n, p] = state[n]

    def finish(t):
        for p in range(2):
            coarse = expand(tuple(st1[n, p, pl.ds(128 * t, 128), :] for n in range(3)), ex)
            num, total, _ = merge(tuple(st0[n, p, pl.ds(BLOCK * t, BLOCK), :] for n in range(3)), coarse)
            at[t, :, 128 * p : 128 * p + 128] = (num / total).astype(BF16)

        @pl.when(x == t)
        def _():
            ra[t] = at[t]

        @pl.when(x != t)
        def _():
            d = lax.rem(t + HEADX - x, HEADX)
            send(at.at[t], ra.at[x], AT + d, i, t)

    finish(1)
    finish(2)

    received(kv0.at[:, :, pl.ds(0, BLOCK)], L0_P)
    received(kv0.at[:, :, pl.ds(5 * BLOCK, BLOCK)], L0_N)

    @pl.loop(0, 4)
    def _(u):
        level0(3 * lax.div(u, 2), lax.rem(u, 2))

    finish(0)
    finish(3)

    load_w.wait()
    for d in range(1, 4):
        received(wbuf.at[lax.rem(x + HEADX - d, HEADX), pl.ds(128 * (1 - core), 128)], WF + d)
    for d in range(1, 4):
        received(ra.at[lax.rem(x + HEADX - d, HEADX)], AT + d)
    for n in range(4):
        columns = pl.ds(256 * n, 256)
        total = jnp.dot(ra[0], wbuf[0, :, columns], preferred_element_type=F32)
        for m in range(1, 4):
            total += jnp.dot(ra[m], wbuf[m, :, columns], preferred_element_type=F32)
        out_ref[:, columns] = total.astype(BF16)

    for copy in sends:
        copy.wait_send()
    sent(r5, KV5)
    sent(r4, KV4)
    sent(r3, KV3)
    for d in range(1, 4):
        sent(at.at[lax.rem(x + d, HEADX)], AT + d)


def packed(first, second, h, low_half):
    lanes = slice(128 * (h // 2), 128 * (h // 2) + 128)
    first = first[:, lanes]
    if h % 2:
        first = pltpu.roll(first, 64, 1)
    if second is None:
        return jnp.where(low_half, first, 0.0)
    second = second[:, lanes]
    if h % 2 == 0:
        second = pltpu.roll(second, 64, 1)
    return jnp.where(low_half, first, second)


def on_device(query_rows, key_rows, value_rows, segment, w_out):
    vmem = pltpu.VMEM
    return pl.pallas_call(
        kernel,
        out_shape=jax.ShapeDtypeStruct((BLOCK, 1024), BF16),
        in_specs=[pl.BlockSpec(memory_space=pl.ANY)] * 5,
        out_specs=pl.BlockSpec(memory_space=vmem),
        scratch_shapes=[
            vmem((2, ROWS, 128), BF16),
            vmem((2, 2, ROWS + 512, 128), BF16),
            vmem((3, 8, 128), jnp.int32),
            vmem((24, 128), F32),
            vmem((2, 512, 128), BF16),
            vmem((2, 2, 1024, 128), BF16),
            vmem((2, 256, 128), BF16),
            vmem((2, 2, 768, 128), BF16),
            vmem((2, 2, 128, 128), BF16),
            vmem((2, 2, 2, 128, 128), BF16),
            vmem((2, 128, 128), BF16),
            vmem((2, 128, 128), BF16),
            vmem((4, 64, 128), BF16),
            vmem((2, 4, 64, 128), BF16),
            vmem((4, 32, 128), BF16),
            vmem((2, 8, 32, 128), BF16),
            vmem((4, 96, 128), BF16),
            vmem((4, 96, 128), BF16),
            vmem((3, 2, ROWS, 128), F32),
            vmem((3, 2, 512, 128), F32),
            vmem((3, 2, 256, 128), F32),
            vmem((2, 3, 128, 128), F32),
            vmem((2, 3, 128, 128), F32),
            vmem((4, 96, 128), F32),
            vmem((4, 96, 128), F32),
            vmem((3, 512, 128), F32),
            vmem((4, BLOCK, 256), BF16),
            vmem((4, BLOCK, 256), BF16),
            vmem((4, 256, 1024), BF16),
            pltpu.SemaphoreType.DMA((8,)),
            pltpu.SemaphoreType.DMA((N_SEM,)),
            pltpu.SemaphoreType.DMA((N_SEM,)),
        ],
        compiler_params=pltpu.CompilerParams(
            collective_id=0, has_side_effects=True, vmem_limit_bytes=48 * 2**20
        ),
        name="block_attention",
    )(query_rows, key_rows, value_rows, segment.reshape(8, 128), w_out)


def solution(mesh):
    placed = (P("seq", "head"), P("seq", "head"), P("seq", "head"), P("seq"), P("head", None))
    return jax.shard_map(
        on_device, mesh=mesh, in_specs=placed, out_specs=P(("seq", "head"), None), check_vma=False
    )
```

time: 632 us -> 56.7 us (0.09); the launches traced: 622 us -> 56.4 us
  starting transfers between devices: 211 us -> 0 us
  waiting for transfers between devices: 202 us -> 0 us
  local copies, waits for them, and re-layouts: 115 us -> 5.65 us
  other arithmetic: 56.9 us -> 0 us
  Pallas kernels: 0 us -> 50.7 us
  matrix products: 20.3 us -> 0 us
  between operations: 16 us -> 0.01 us
    ppermute x54 -> x0, starting transfers between devices: 211 us -> none  [the longest x50 198 us: from_behind(): return lax.ppermute(array, axis, pairs)]
    ppermute x54 -> x0, waiting for transfers between devices: 137 us -> none  [the longest x50 137 us: from_behind(): return lax.ppermute(array, axis, pairs)]
    reduce_scatter x1 -> x0, waiting for transfers between devices: 65.1 us -> none  [on_device(): lax.psum_scatter(jnp.dot(attention, w_out, preferred_element_type=jnp.flo...]
    pallas_call x0 -> x1, Pallas kernels: none -> 50.7 us  [on_device(): pl.pallas_call(kernel, out_shape=jax.ShapeDtypeStruct((BLOCK, 1024), BF16...]
    reshape x33 -> x0, local copies, waits for them, and re-layouts: 48.4 us -> none  [the longest x10 23.7 us: on_device(): weighted = jnp.repeat(weighted, factor, axis=0)]
    reduce_sum x22 -> x0, other arithmetic: 24.9 us -> none  [the longest x15 16.2 us: on_device(): jnp.mean(source.reshape(half_rows, 2, feat_count), axis=1)]
    dot_general x15 -> x0, matrix products: 20.3 us -> none  [the longest x7 11 us: block_attend(): jnp.einsum('nhqk,nkhd->nqhd', weights.astype(jnp.bfloat16), value_block,...]
    convert_element_type x16 -> x0, other arithmetic: 15.5 us -> none  [the longest x5 8.16 us: on_device(): coarse_q.append(current[0].astype(jnp.bfloat16))]
  transfers between devices with their start and end apart: 55 -> 0, of which waited for: 35 -> 0; matrix products, arithmetic and copies ran while one was open for 14% -> 0% of each run, Pallas kernels for 0% -> 0%
where the time goes in v1:
time: 56.7 us; the launch traced here: 56.4 us
  Pallas kernels  50.7 us (89%)
  local copies, waits for them, and re-layouts  5.65 us (10%)
    pallas_call x1, Pallas kernels, on_device(): pl.pallas_call(kernel, out_shape=jax.ShapeDtypeStruct((BLOCK, 1024), BF16...  50.7 us
    unnamed x11, local copies, waits for them, and re-layouts  5.65 us

profile of v1, /device:TPU:1, one launch (start us, length us, event | category | flops | bytes accessed | tf_op | source)
XLA Modules:
  0.0 56.4 jit_solution(5936413640563288418)
XLA Ops:
  0.0 0.0 copy-start
  0.0 1.0 %copy-done = bf16[1024,256]{1,0:T(8,128)(2,1)S(1)} copy-done((bf16[1024,256]{1,0:T(8,128)(2,1)S(1)}, bf16[1024,256]{1,0:T(8,128)(2,1)}, u32[]{:S(2)}) %copy-start) | copy-done | bytes 524312
  1.0 0.0 copy-start.1
  1.0 1.0 %copy-done.1 = bf16[1024,256]{1,0:T(8,128)(2,1)S(1)} copy-done((bf16[1024,256]{1,0:T(8,128)(2,1)S(1)}, bf16[1024,256]{1,0:T(8,128)(2,1)}, u32[]{:S(2)}) %copy-start.1) | copy-done | bytes 524312
  2.1 0.0 copy-start.2
  2.1 1.0 %copy-done.2 = bf16[1024,256]{1,0:T(8,128)(2,1)S(1)} copy-done((bf16[1024,256]{1,0:T(8,128)(2,1)S(1)}, bf16[1024,256]{1,0:T(8,128)(2,1)}, u32[]{:S(2)}) %copy-start.2) | copy-done | bytes 524312
  3.1 0.0 copy-start.3
  3.1 1.0 %copy-done.3 = bf16[256,1024]{1,0:T(8,128)(2,1)S(1)} copy-done((bf16[256,1024]{1,0:T(8,128)(2,1)S(1)}, bf16[256,1024]{1,0:T(8,128)(2,1)}, u32[]{:S(2)}) %copy-start.3) | copy-done | bytes 524312
  4.2 0.0 copy-start.4
  4.2 0.7 %copy-done.4 = s32[1024]{0:T(1024)S(1)} copy-done((s32[1024]{0:T(1024)S(1)}, s32[1024]{0:T(1024)}, u32[]{:S(2)}) %copy-start.4) | copy-done | bytes 4120
  4.9 50.7 %block_attention.1 = bf16[256,1024]{1,0:T(8,128)(2,1)S(1)} custom-call(bf16[1024,256]{1,0:T(8,128)(2,1)S(1)} %copy-done, bf16[1024,256]{1,0:T(8,128)(2,1)S(1)} %copy-done.1, bf16[1024,256]{1,0:T(8,128)(2,1)S(1)} %copy-done.2, s32[8,128]{1,0:T(8,128)S(1)} %bitcast.1, bf16[256,1024]{1,0:T(8,128)(2,1)S(1)} %copy-done.3), custom_call_target="tpu_custom_call" | custom-call | tf_op jit(solution)/shard_map/block_attention/pallas_call | solution.py:399
  55.6 0.8 %copy.7 = bf16[256,1024]{1,0:T(8,128)(2,1)} copy(bf16[256,1024]{1,0:T(8,128)(2,1)S(1)} %block_attention.1) | data formatting | bytes 1048576
Async XLA Ops:
  0.0 1.0 %copy-start = (bf16[1024,256]{1,0:T(8,128)(2,1)S(1)}, bf16[1024,256]{1,0:T(8,128)(2,1)}, u32[]{:S(2)}) copy-start(bf16[1024,256]{1,0:T(8,128)(2,1)} %q_hbm.1) | copy-start | bytes 1572868
  1.0 1.0 %copy-start.1 = (bf16[1024,256]{1,0:T(8,128)(2,1)S(1)}, bf16[1024,256]{1,0:T(8,128)(2,1)}, u32[]{:S(2)}) copy-start(bf16[1024,256]{1,0:T(8,128)(2,1)} %k_hbm.1) | copy-start | bytes 1572868
  2.1 1.0 %copy-start.2 = (bf16[1024,256]{1,0:T(8,128)(2,1)S(1)}, bf16[1024,256]{1,0:T(8,128)(2,1)}, u32[]{:S(2)}) copy-start(bf16[1024,256]{1,0:T(8,128)(2,1)} %v_hbm.1) | copy-start | bytes 1572868
  3.1 1.0 %copy-start.3 = (bf16[256,1024]{1,0:T(8,128)(2,1)S(1)}, bf16[256,1024]{1,0:T(8,128)(2,1)}, u32[]{:S(2)}) copy-start(bf16[256,1024]{1,0:T(8,128)(2,1)} %w_hbm.1) | copy-start | bytes 1572868
  4.2 0.7 %copy-start.4 = (s32[1024]{0:T(1024)S(1)}, s32[1024]{0:T(1024)}, u32[]{:S(2)}) copy-start(s32[1024]{0:T(1024)} %param.8) | copy-start | bytes 12292

commit v2 on v1

--- a/solution.py
+++ b/solution.py
@@ -17,9 +17,13 @@
 BIG = 1e30
 
 SEG_P, SEG_N, L0_P, L0_N, L1_P, L1_N, L2_P, L2_N = range(8)
-KV3, KV4, KV5, Q3, RES3 = range(8, 13)
-Q45, RES45, WG, WF, AT = 12, 15, 18, 21, 24
-N_SEM = 28
+KV3, KV4, KV5, KV5_Y, Q3, Q5, RES3, RES5 = range(8, 16)
+Q4, RES4 = 15, 18
+W_L, W_R, W2_L, W2_R, W_ON_L, W_ON_R, W_ON_2 = range(22, 29)
+AT_L, AT_R, VIA, AT_2 = 29, 31, 33, 35
+N_SEM = 37
+
+OWNER5 = (0, 1, 6, 7)
 
 
 def averaging():
@@ -85,8 +89,8 @@
 def kernel(
     q_hbm, k_hbm, v_hbm, seg_hbm, w_hbm, out_ref,
     q0, kv0, segi, segf, q1, kv1, q2, kv2,
-    s3, r3, sq3, rq3, s4, r4, s5, r5, sq45, rq45,
-    st0, st1, st2, st3, rs3, srow, rrow, ex, at, ra, wbuf,
+    s3, r3, sq3, rq3, s4, r4, s5, r5, sq4, rq4, sq5, rq5,
+    st0, st1, st2, st3, rs3, srow4, rrow4, srow5, rrow5, ex, at, ra, via, wbuf,
     local, snd, rcv,
 ):
     i = lax.axis_index("seq")
@@ -97,6 +101,12 @@
     g5, a5 = lax.div(i, 8), lax.rem(i, 8)
     sibling = i + 1 - 2 * core
     right, left = lax.rem(i + 1, SEQ), lax.rem(i + SEQ - 1, SEQ)
+    x_up, x_down, x_far = [lax.rem(x + d, HEADX) for d in (1, 3, 2)]
+    late = lax.rem(g5, 2)
+    beside5 = g5 + 1 - 2 * late
+    owner5 = (a5 < 2) | (a5 >= 6)
+    head5 = jnp.where(a5 < 2, a5, lax.rem(a5, 4))
+    y_on = lax.rem(i + SEQ + 16 - 32 * late, SEQ)
 
     def remote(src, dst, slot, device):
         return pltpu.make_async_remote_copy(
@@ -121,16 +131,17 @@
         pl.semaphore_signal(barrier, inc=1, device_id={"seq": seq, "head": head}, device_id_type=MESH)
 
     blocks4 = [lax.rem(g4 + 1, SEQ // 4), lax.rem(g4 + SEQ // 4 - 1, SEQ // 4)]
-    blocks5 = [lax.rem(g5 + 1, SEQ // 8), lax.rem(g5 + SEQ // 8 - 1, SEQ // 8)]
-    for block in blocks5:
-        for j in range(8):
-            greet(block * 8 + j, x)
+    for j in range(8):
+        greet(beside5 * 8 + j, x)
     for block in blocks4:
         for j in range(4):
             greet(block * 4 + j, x)
-    for d in range(1, 4):
-        greet(g4 * 4 + lax.rem(a4 + d, 4), x)
-        greet(i, lax.rem(x + d, HEADX))
+    for d in range(1, 8):
+        greet(g5 * 8 + lax.rem(a5 + d, 8), x)
+    for other in (x_up, x_down):
+        greet(i, other)
+    greet(lax.rem(i + 16, SEQ), x)
+    greet(lax.rem(i + SEQ - 16, SEQ), x)
 
     lane = lax.broadcasted_iota(jnp.int32, (1, 128), 1)
     low_half = lane < 64
@@ -160,62 +171,16 @@
                 s3[p, n, pl.ds(32 * t, 32), :] = c[192:224, lanes].astype(BF16)
         for h in range(4):
             s4[h, pl.ds(16 * t, 16), :] = packed(ck[224:240], cv[224:240], h, low_half).astype(BF16)
-            sq45[h, pl.ds(16 * t, 16), :] = packed(cq[224:240], None, h, low_half).astype(BF16)
+            sq4[h, pl.ds(16 * t, 16), :] = packed(cq[224:240], None, h, low_half).astype(BF16)
         last_k.append(ck[240:248])
         last_v.append(cv[240:248])
         last_q.append(cq[240:248])
     k5, v5, q5 = [jnp.concatenate(rows, axis=0) for rows in (last_k, last_v, last_q)]
     for h in range(4):
         s5[h] = packed(k5, v5, h, low_half).astype(BF16)
-        sq45[h, pl.ds(64, 32), :] = packed(q5, None, h, low_half).astype(BF16)
-
-    pl.semaphore_wait(barrier, 30)
-    sends = []
-
-    def send(src, dst, slot, seq, head=x):
-        copy = remote(src, dst, slot, {"seq": seq, "head": head})
-        copy.start()
-        return copy
-
-    half = pl.ds(128 * core, 128)
-    for d in (1, 3, 2):
-        sends.append(send(w_hbm.at[half], wbuf.at[x, half], WG + d, i, lax.rem(x + d, HEADX)))
-    sends.append(send(sq3.at[1 - core], rq3.at[core], Q3, sibling))
-    for d in range(1, 4):
-        other = lax.rem(a4 + d, 4)
-        sends.append(send(sq45.at[other], rq45.at[a4], Q45 + d, g4 * 4 + other))
-    for direction, block in enumerate(blocks5):
-        for j in range(8):
-            send(s5.at[j % 4], r5.at[direction, a5], KV5, block * 8 + j)
-    for direction, block in enumerate(blocks4):
-        for j in range(4):
-            send(s4.at[j], r4.at[direction, a4], KV4, block * 4 + j)
-    for direction, by in enumerate((1, SEQ // 2 - 1)):
-        beside = lax.rem(chip + by, SEQ // 2)
-        for p in range(2):
-            send(s3.at[p], r3.at[direction, :, core], KV3, beside * 2 + p)
-    sends.append(send(segi.at[1], segi.at[0], SEG_P, right))
-    sends.append(send(segi.at[1], segi.at[2], SEG_N, left))
-    for ref, count, slot in ((kv2, 256, L2_P), (kv1, 512, L1_P), (kv0, 1024, L0_P)):
-        sends.append(
-            send(ref.at[:, :, pl.ds(count, BLOCK)], ref.at[:, :, pl.ds(0, BLOCK)], slot, right)
-        )
-        sends.append(
-            send(ref.at[:, :, pl.ds(BLOCK, BLOCK)], ref.at[:, :, pl.ds(BLOCK + count, BLOCK)], slot + 1, left)
-        )
-    rq3[core] = sq3[core]
-    rq45[a4] = sq45[a4]
-
-    def received(ref, slot):
-        pltpu.make_async_copy(ref, ref, rcv.at[slot]).wait()
-
-    def sent(ref, slot):
-        pltpu.make_async_copy(ref, ref, snd.at[slot]).wait()
-
-    received(segi.at[0], SEG_P)
-    received(segi.at[2], SEG_N)
-    for n in range(3):
-        segf[pl.ds(8 * n, 8), :] = segi[n].astype(F32)
+        sq5[h] = packed(q5, None, h, low_half).astype(BF16)
+
+    segf[pl.ds(8, 8), :] = segi[1].astype(F32)
 
     def bias_of(b, j):
         exists = (4 * i + b + j >= 1) & (4 * i + b + j <= 4 * SEQ)
@@ -240,41 +205,117 @@
         for n in range(3):
             st0[n, p, pl.ds(pl.multiple_of(b * BLOCK, BLOCK), BLOCK), :] = state[n]
 
-    @pl.loop(0, 4)
-    def _(u):
-        level0(1 + lax.div(u, 2), lax.rem(u, 2))
-
-    for d in (1, 3, 2):
-        owner = lax.rem(x + HEADX - d, HEADX)
-        received(wbuf.at[owner, half], WG + d)
-        sends.append(send(wbuf.at[owner, half], wbuf.at[owner, half], WF + d, sibling))
-
-    for d in range(1, 4):
-        received(rq45.at[lax.rem(a4 + 4 - d, 4)], Q45 + d)
-
-    def one_head(ref, queries, first, rows, place, count):
-        block_rows = ref.shape[1] * ref.shape[2]
-        tiles = [ref[n].reshape(block_rows, 128) for n in range(2)]
-        out, peak = attend(queries, tiles, [t * hi + lo for t in tiles], None, (place > 0, place < count - 1))
-        out = jnp.where((lane >= 32) & low_half, peak, out)
-        for n in range(4):
-            srow[n, pl.ds(first, rows), :] = out[n * rows : (n + 1) * rows]
-
-    received(r5, KV5)
-    one_head(r5, rq45[:, 64:96, :].reshape(128, 128), 64, 32, g5, SEQ // 8)
-    received(r4, KV4)
-    one_head(r4, rq45[:, 0:64, :].reshape(256, 128), 0, 64, g4, SEQ // 4)
+    @pl.when(late == 0)
+    def _():
+        @pl.loop(0, 4)
+        def _(u):
+            level0(1 + lax.div(u, 2), lax.rem(u, 2))
+
+    pl.semaphore_wait(barrier, 27)
+    sends = []
+
+    def send(src, dst, slot, seq, head=x):
+        copy = remote(src, dst, slot, {"seq": seq, "head": head})
+        copy.start()
+        return copy
+
+    def received(ref, slot):
+        pltpu.make_async_copy(ref, ref, rcv.at[slot]).wait()
+
+    def sent(ref, slot):
+        pltpu.make_async_copy(ref, ref, snd.at[slot]).wait()
+
+    def to_sides(ref, count, skip, slot):
+        n = BLOCK - skip
+        sends.append(send(ref.at[:, :, pl.ds(count, n)], ref.at[:, :, pl.ds(0, n)], slot, right))
+        sends.append(
+            send(
+                ref.at[:, :, pl.ds(BLOCK + skip, n)], ref.at[:, :, pl.ds(BLOCK + count + skip, n)], slot + 1, left
+            )
+        )
+
+    half = pl.ds(128 * core, 128)
+    sends.append(send(w_hbm.at[half], wbuf.at[x, half], W_L, i, x_up))
+    sends.append(send(w_hbm.at[half], wbuf.at[x, half], W_R, i, x_down))
+    for h in range(4):
+        send(s5.at[h], r5.at[late, a5], KV5, beside5 * 8 + OWNER5[h])
+
+        @pl.when(a5 != OWNER5[h])
+        def _():
+            send(sq5.at[h], rq5.at[a5], Q5, g5 * 8 + OWNER5[h])
+
+        @pl.when(a5 == OWNER5[h])
+        def _():
+            rq5[a5] = sq5[h]
+
+    for direction, block in enumerate(blocks4):
+        for j in range(4):
+            send(s4.at[j], r4.at[direction, a4], KV4, block * 4 + j)
     for d in range(1, 4):
         other = lax.rem(a4 + d, 4)
-        sends.append(send(srow.at[other], rrow.at[a4], RES45 + d, g4 * 4 + other))
-    rrow[a4] = srow[a4]
+        sends.append(send(sq4.at[other], rq4.at[a4], Q4 + d, g4 * 4 + other))
+    sends.append(send(sq3.at[1 - core], rq3.at[core], Q3, sibling))
+    for direction, by in enumerate((1, SEQ // 2 - 1)):
+        beside = lax.rem(chip + by, SEQ // 2)
+        for p in range(2):
+            send(s3.at[p], r3.at[direction, :, core], KV3, beside * 2 + p)
+    sends.append(send(segi.at[1], segi.at[0], SEG_P, right))
+    sends.append(send(segi.at[1], segi.at[2], SEG_N, left))
+    to_sides(kv0, ROWS, 0, L0_P)
+    to_sides(kv2, 256, 64, L2_P)
+    to_sides(kv1, 512, 128, L1_P)
+    rq3[core] = sq3[core]
+    rq4[a4] = sq4[a4]
+
+    @pl.when(late == 1)
+    def _():
+        @pl.loop(0, 4)
+        def _(u):
+            level0(1 + lax.div(u, 2), lax.rem(u, 2))
+
+    @pl.when(owner5)
+    def _():
+        received(r5.at[1 - late], KV5)
+        send(r5.at[1 - late], r5.at[late], KV5_Y, y_on)
+
+    quarter = [pl.ds(128 * core, 64), pl.ds(128 * core + 64, 64)]
+    received(wbuf.at[x_down, half], W_L)
+    sends.append(send(wbuf.at[x_down, quarter[0]], wbuf.at[x_down, quarter[0]], W2_L, i, x_up))
+    sends.append(send(wbuf.at[x_down, half], wbuf.at[x_down, half], W_ON_L, sibling))
+    received(wbuf.at[x_up, half], W_R)
+    sends.append(send(wbuf.at[x_up, quarter[1]], wbuf.at[x_up, quarter[1]], W2_R, i, x_down))
+    sends.append(send(wbuf.at[x_up, half], wbuf.at[x_up, half], W_ON_R, sibling))
+
+    def one_head(ref, queries, place, count):
+        tiles = [ref[n].reshape(BLOCK, 128) for n in range(2)]
+        out, peak = attend(queries, tiles, [t * hi + lo for t in tiles], None, (place > 0, place < count - 1))
+        return jnp.where((lane >= 32) & low_half, peak, out)
+
+    for d in range(1, 4):
+        received(rq4.at[lax.rem(a4 + 4 - d, 4)], Q4 + d)
+    received(r4, KV4)
+    srow4[...] = one_head(r4, rq4[...].reshape(BLOCK, 128), g4, SEQ // 4).reshape(4, 64, 128)
+    for d in range(1, 4):
+        other = lax.rem(a4 + d, 4)
+        sends.append(send(srow4.at[other], rrow4.at[a4], RES4 + d, g4 * 4 + other))
+    rrow4[a4] = srow4[a4]
+
+    @pl.when(owner5)
+    def _():
+        received(rq5.at[pl.ds(0, 7)], Q5)
+        received(r5.at[late], KV5_Y)
+        srow5[...] = one_head(r5, rq5[...].reshape(BLOCK, 128), g5, SEQ // 8).reshape(8, 32, 128)
+        for d in range(1, 8):
+            other = lax.rem(a5 + d, 8)
+            send(srow5.at[other], rrow5.at[head5], RES5, g5 * 8 + other)
+        rrow5[head5] = srow5[a5]
 
     received(r3, KV3)
     received(rq3.at[1 - core], Q3)
     state = pair(
-        rq3[...].reshape(256, 128),
-        [r3[n, 0].reshape(256, 128) for n in range(2)],
-        [r3[n, 1].reshape(256, 128) for n in range(2)],
+        rq3[...].reshape(BLOCK, 128),
+        [r3[n, 0].reshape(BLOCK, 128) for n in range(2)],
+        [r3[n, 1].reshape(BLOCK, 128) for n in range(2)],
         None,
         (chip > 0, chip < SEQ // 2 - 1),
         low_half, lo, hi,
@@ -285,8 +326,21 @@
     sends.append(send(rs3.at[1 - core], st3.at[core], RES3, sibling))
     st3[core] = rs3[core]
 
-    received(kv2.at[:, :, pl.ds(0, BLOCK)], L2_P)
-    received(kv2.at[:, :, pl.ds(2 * BLOCK, BLOCK)], L2_N)
+    received(segi.at[0], SEG_P)
+    received(segi.at[2], SEG_N)
+    segf[pl.ds(0, 8), :] = segi[0].astype(F32)
+    segf[pl.ds(16, 8), :] = segi[2].astype(F32)
+    for side, (first, row1, row2) in enumerate(((0, 128, 192), (5 * BLOCK, 3 * BLOCK, 2 * BLOCK))):
+        received(kv0.at[:, :, pl.ds(first, BLOCK)], L0_P + side)
+        for n in range(2):
+            rim = jnp.concatenate([kv0[n, p, pl.ds(first, BLOCK), :] for p in range(2)], axis=1)
+            rim = jnp.dot(means[:192], rim, preferred_element_type=F32).astype(BF16)
+            for p in range(2):
+                kv1[n, p, pl.ds(row1, 128), :] = rim[:128, 128 * p : 128 * p + 128]
+                kv2[n, p, pl.ds(row2, 64), :] = rim[128:, 128 * p : 128 * p + 128]
+
+    received(kv2.at[:, :, pl.ds(0, 192)], L2_P)
+    received(kv2.at[:, :, pl.ds(2 * BLOCK + 64, 192)], L2_N)
 
     @pl.loop(0, 2)
     def _(p):
@@ -298,8 +352,8 @@
         for n in range(3):
             st2[n, p] = state[n]
 
-    received(kv1.at[:, :, pl.ds(0, BLOCK)], L1_P)
-    received(kv1.at[:, :, pl.ds(3 * BLOCK, BLOCK)], L1_N)
+    received(kv1.at[:, :, pl.ds(0, 128)], L1_P)
+    received(kv1.at[:, :, pl.ds(3 * BLOCK + 128, 128)], L1_N)
 
     @pl.loop(0, 4)
     def _(u):
@@ -314,71 +368,110 @@
         for n in range(3):
             st1[n, p, own, :] = state[n]
 
+    received(wbuf.at[x_far, quarter[0]], W2_L)
+    received(wbuf.at[x_far, quarter[1]], W2_R)
+    sends.append(send(wbuf.at[x_far, half], wbuf.at[x_far, half], W_ON_2, sibling))
+
     for d in range(1, 4):
-        received(rrow.at[lax.rem(a4 + 4 - d, 4)], RES45 + d)
+        received(rrow4.at[lax.rem(a4 + 4 - d, 4)], RES4 + d)
+
+    @pl.when(owner5)
+    def _():
+        received(rrow5.at[pl.ds(0, 3)], RES5)
+
+    @pl.when(jnp.logical_not(owner5))
+    def _():
+        received(rrow5, RES5)
+
     received(st3.at[1 - core], RES3)
     for p in range(2):
 
-        def far(rows):
-            even, odd = rrow[2 * p, rows, :], rrow[2 * p + 1, rows, :]
+        def far(ref):
+            even, odd = ref[2 * p], ref[2 * p + 1]
             num = jnp.where(low_half, pltpu.roll(even, 64, 1), odd)
             total = jnp.where(low_half, even[:, 0:1], odd[:, 0:1])
             return num, total, jnp.where(low_half, even[:, 32:33], odd[:, 32:33])
 
-        state = merge(expand(far(slice(64, 96)), ex), far(slice(0, 64)))
+        state = merge(expand(far(rrow5), ex), far(rrow4))
         state = merge(expand(state, ex), tuple(st3[p, n] for n in range(3)))
         state = merge(expand(state, ex), tuple(st2[n, p] for n in range(3)))
         state = merge(expand(state, ex), tuple(st1[n, p] for n in range(3)))
         for n in range(3):
             st1[n, p] = state[n]
 
-    def finish(t):
+    def finish(t, p):
+        coarse = expand(tuple(st1[n, p, pl.ds(pl.multiple_of(128 * t, 128), 128), :] for n in range(3)), ex)
+        fine = tuple(st0[n, p, pl.ds(pl.multiple_of(BLOCK * t, BLOCK), BLOCK), :] for n in range(3))
+        num, total, _ = merge(fine, coarse)
+        attention = (num / total).astype(BF16)
+        d = lax.rem(t + HEADX - x, HEADX)
+        at[t, p] = attention
+
+        @pl.when(d == 0)
+        def _():
+            ra[x, p] = attention
+
+        @pl.when(d == 1)
+        def _():
+            send(at.at[t, p], ra.at[x, p], AT_L + p, i, x_up)
+
+        @pl.when(d == 3)
+        def _():
+            send(at.at[t, p], ra.at[x, p], AT_R + p, i, x_down)
+
+        @pl.when(d == 2)
+        def _():
+            send(at.at[t, p], via.at[p], VIA + p, i, x_down if p else x_up)
+
+    for t in (1, 2):
         for p in range(2):
-            coarse = expand(tuple(st1[n, p, pl.ds(128 * t, 128), :] for n in range(3)), ex)
-            num, total, _ = merge(tuple(st0[n, p, pl.ds(BLOCK * t, BLOCK), :] for n in range(3)), coarse)
-            at[t, :, 128 * p : 128 * p + 128] = (num / total).astype(BF16)
-
-        @pl.when(x == t)
-        def _():
-            ra[t] = at[t]
-
-        @pl.when(x != t)
-        def _():
-            d = lax.rem(t + HEADX - x, HEADX)
-            send(at.at[t], ra.at[x], AT + d, i, t)
-
-    finish(1)
-    finish(2)
-
-    received(kv0.at[:, :, pl.ds(0, BLOCK)], L0_P)
-    received(kv0.at[:, :, pl.ds(5 * BLOCK, BLOCK)], L0_N)
-
-    @pl.loop(0, 4)
-    def _(u):
-        level0(3 * lax.div(u, 2), lax.rem(u, 2))
-
-    finish(0)
-    finish(3)
+            finish(t, p)
+
+    first = jnp.where(x < 2, 3, 0)
+    for t in (first, 3 - first):
+        for p in range(2):
+            level0(t, p)
+            finish(t, p)
+    received(via.at[0], VIA)
+    sends.append(send(via.at[0], ra.at[x_down, 0], AT_2, i, x_up))
+    received(via.at[1], VIA + 1)
+    sends.append(send(via.at[1], ra.at[x_up, 1], AT_2 + 1, i, x_down))
 
     load_w.wait()
-    for d in range(1, 4):
-        received(wbuf.at[lax.rem(x + HEADX - d, HEADX), pl.ds(128 * (1 - core), 128)], WF + d)
-    for d in range(1, 4):
-        received(ra.at[lax.rem(x + HEADX - d, HEADX)], AT + d)
+    other_half = pl.ds(128 * (1 - core), 128)
+    for owner, slot in ((x_down, W_ON_L), (x_up, W_ON_R), (x_far, W_ON_2)):
+        received(wbuf.at[owner, other_half], slot)
+    for p in range(2):
+        for owner, slot in ((x_down, AT_L), (x_up, AT_R), (x_far, AT_2)):
+            received(ra.at[owner, p], slot + p)
     for n in range(4):
         columns = pl.ds(256 * n, 256)
-        total = jnp.dot(ra[0], wbuf[0, :, columns], preferred_element_type=F32)
-        for m in range(1, 4):
-            total += jnp.dot(ra[m], wbuf[m, :, columns], preferred_element_type=F32)
+        total = None
+        for m in range(4):
+            rows = jnp.concatenate([ra[m, 0], ra[m, 1]], axis=1)
+            part = jnp.dot(rows, wbuf[m, :, columns], preferred_element_type=F32)
+            total = part if total is None else total + part
         out_ref[:, columns] = total.astype(BF16)
 
     for copy in sends:
         copy.wait_send()
-    sent(r5, KV5)
+    sent(s5, KV5)
+    for h in range(4):
+
+        @pl.when(a5 != OWNER5[h])
+        def _():
+            sent(sq5.at[h], Q5)
+
+    @pl.when(owner5)
+    def _():
+        sent(r5.at[0], KV5_Y)
+        sent(srow5.at[pl.ds(0, 7)], RES5)
+
     sent(r4, KV4)
     sent(r3, KV3)
-    for d in range(1, 4):
-        sent(at.at[lax.rem(x + d, HEADX)], AT + d)
+    for p in range(2):
+        for slot in (AT_L, AT_R, VIA):
+            sent(at.at[0, p], slot + p)
 
 
 def packed(first, second, h, low_half):
@@ -418,25 +511,30 @@
             vmem((2, 4, 64, 128), BF16),
             vmem((4, 32, 128), BF16),
             vmem((2, 8, 32, 128), BF16),
-            vmem((4, 96, 128), BF16),
-            vmem((4, 96, 128), BF16),
+            vmem((4, 64, 128), BF16),
+            vmem((4, 64, 128), BF16),
+            vmem((4, 32, 128), BF16),
+            vmem((8, 32, 128), BF16),
             vmem((3, 2, ROWS, 128), F32),
             vmem((3, 2, 512, 128), F32),
             vmem((3, 2, 256, 128), F32),
             vmem((2, 3, 128, 128), F32),
             vmem((2, 3, 128, 128), F32),
-            vmem((4, 96, 128), F32),
-            vmem((4, 96, 128), F32),
+            vmem((4, 64, 128), F32),
+            vmem((4, 64, 128), F32),
+            vmem((8, 32, 128), F32),
+            vmem((4, 32, 128), F32),
             vmem((3, 512, 128), F32),
-            vmem((4, BLOCK, 256), BF16),
-            vmem((4, BLOCK, 256), BF16),
+            vmem((4, 2, BLOCK, 128), BF16),
+            vmem((4, 2, BLOCK, 128), BF16),
+            vmem((2, BLOCK, 128), BF16),
             vmem((4, 256, 1024), BF16),
             pltpu.SemaphoreType.DMA((8,)),
             pltpu.SemaphoreType.DMA((N_SEM,)),
             pltpu.SemaphoreType.DMA((N_SEM,)),
         ],
         compiler_params=pltpu.CompilerParams(
-            collective_id=0, has_side_effects=True, vmem_limit_bytes=48 * 2**20
+            collective_id=0, has_side_effects=True, vmem_limit_bytes=62 * 2**20
         ),
         name="block_attention",
     )(query_rows, key_rows, value_rows, segment.reshape(8, 128), w_out)

time: 56.7 us -> 49.5 us (0.87)
  local copies, waits for them, and re-layouts: 5.65 us -> 1.87 us
  Pallas kernels: 50.7 us -> 47.5 us
    unnamed x11 -> x1, local copies, waits for them, and re-layouts: 5.65 us -> 1.87 us
    pallas_call x1, Pallas kernels: 50.7 us -> 47.5 us  [on_device(): pl.pallas_call(kernel, out_shape=jax.ShapeDtypeStruct((BLOCK, 1024), BF16...]
where the time goes in v2:
time: 49.5 us; the launch traced here: 49.4 us
  Pallas kernels  47.5 us (96%)
  local copies, waits for them, and re-layouts  1.87 us (4%)
    pallas_call x1, Pallas kernels, on_device(): pl.pallas_call(kernel, out_shape=jax.ShapeDtypeStruct((BLOCK, 1024), BF16...  47.5 us
    unnamed x1, local copies, waits for them, and re-layouts  1.87 us

profile of v2, /device:TPU:1, one launch (start us, length us, event | category | flops | bytes accessed | tf_op | source)
XLA Modules:
  0.0 49.4 jit_solution(16299455249590277805)
XLA Ops:
  0.0 47.5 %block_attention.1 = bf16[256,1024]{1,0:T(8,128)(2,1)} custom-call(bf16[1024,256]{1,0:T(8,128)(2,1)} %q_hbm.1, bf16[1024,256]{1,0:T(8,128)(2,1)} %k_hbm.1, bf16[1024,256]{1,0:T(8,128)(2,1)} %v_hbm.1, s32[8,128]{1,0:T(8,128)} %bitcast.1, bf16[256,1024]{1,0:T(8,128)(2,1)} %w_hbm.1), custom_call_target="tpu_custom_call" | custom-call | tf_op jit(solution)/shard_map/block_attention/pallas_call | solution.py:492
  47.5 1.9 %copy.7 = bf16[256,1024]{1,0:T(8,128)(2,1)} copy(bf16[256,1024]{1,0:T(8,128)(2,1)} %block_attention.1) | data formatting | bytes 1048576

commit v3 on v2

--- a/solution.py
+++ b/solution.py
@@ -21,7 +21,8 @@
 Q4, RES4 = 15, 18
 W_L, W_R, W2_L, W2_R, W_ON_L, W_ON_R, W_ON_2 = range(22, 29)
 AT_L, AT_R, VIA, AT_2 = 29, 31, 33, 35
-N_SEM = 37
+STAT, FAR = 36, 39
+N_SEM = 43
 
 OWNER5 = (0, 1, 6, 7)
 
@@ -90,7 +91,7 @@
     q_hbm, k_hbm, v_hbm, seg_hbm, w_hbm, out_ref,
     q0, kv0, segi, segf, q1, kv1, q2, kv2,
     s3, r3, sq3, rq3, s4, r4, s5, r5, sq4, rq4, sq5, rq5,
-    st0, st1, st2, st3, rs3, srow4, rrow4, srow5, rrow5, ex, at, ra, via, wbuf,
+    st0, st1, st2, st3, rs3, srow4, rrow4, srow5, rrow5, ex, at, ra, via, sstat, rstat, sfar, rfar, near, wbuf,
     local, snd, rcv,
 ):
     i = lax.axis_index("seq")
@@ -138,7 +139,7 @@
             greet(block * 4 + j, x)
     for d in range(1, 8):
         greet(g5 * 8 + lax.rem(a5 + d, 8), x)
-    for other in (x_up, x_down):
+    for other in (x_up, x_down, x_far):
         greet(i, other)
     greet(lax.rem(i + 16, SEQ), x)
     greet(lax.rem(i + SEQ - 16, SEQ), x)
@@ -211,7 +212,7 @@
         def _(u):
             level0(1 + lax.div(u, 2), lax.rem(u, 2))
 
-    pl.semaphore_wait(barrier, 27)
+    pl.semaphore_wait(barrier, 28)
     sends = []
 
     def send(src, dst, slot, seq, head=x):
@@ -248,6 +249,11 @@
         def _():
             rq5[a5] = sq5[h]
 
+    sends.append(send(segi.at[1], segi.at[0], SEG_P, right))
+    sends.append(send(segi.at[1], segi.at[2], SEG_N, left))
+    to_sides(kv0, ROWS, 0, L0_P)
+    to_sides(kv2, 256, 64, L2_P)
+    to_sides(kv1, 512, 128, L1_P)
     for direction, block in enumerate(blocks4):
         for j in range(4):
             send(s4.at[j], r4.at[direction, a4], KV4, block * 4 + j)
@@ -259,11 +265,6 @@
         beside = lax.rem(chip + by, SEQ // 2)
         for p in range(2):
             send(s3.at[p], r3.at[direction, :, core], KV3, beside * 2 + p)
-    sends.append(send(segi.at[1], segi.at[0], SEG_P, right))
-    sends.append(send(segi.at[1], segi.at[2], SEG_N, left))
-    to_sides(kv0, ROWS, 0, L0_P)
-    to_sides(kv2, 256, 64, L2_P)
-    to_sides(kv1, 512, 128, L1_P)
     rq3[core] = sq3[core]
     rq4[a4] = sq4[a4]
 
@@ -285,6 +286,98 @@
     received(wbuf.at[x_up, half], W_R)
     sends.append(send(wbuf.at[x_up, quarter[1]], wbuf.at[x_up, quarter[1]], W2_R, i, x_down))
     sends.append(send(wbuf.at[x_up, half], wbuf.at[x_up, half], W_ON_R, sibling))
+
+    received(segi.at[0], SEG_P)
+    received(segi.at[2], SEG_N)
+    segf[pl.ds(0, 8), :] = segi[0].astype(F32)
+    segf[pl.ds(16, 8), :] = segi[2].astype(F32)
+    for side, (first, row1, row2) in enumerate(((0, 128, 192), (5 * BLOCK, 3 * BLOCK, 2 * BLOCK))):
+        received(kv0.at[:, :, pl.ds(first, BLOCK)], L0_P + side)
+        for n in range(2):
+            rim = jnp.concatenate([kv0[n, p, pl.ds(first, BLOCK), :] for p in range(2)], axis=1)
+            rim = jnp.dot(means[:192], rim, preferred_element_type=F32).astype(BF16)
+            for p in range(2):
+                kv1[n, p, pl.ds(row1, 128), :] = rim[:128, 128 * p : 128 * p + 128]
+                kv2[n, p, pl.ds(row2, 64), :] = rim[128:, 128 * p : 128 * p + 128]
+
+    received(kv2.at[:, :, pl.ds(0, 192)], L2_P)
+    received(kv2.at[:, :, pl.ds(2 * BLOCK + 64, 192)], L2_N)
+
+    @pl.loop(0, 2)
+    def _(p):
+        sides = [pl.ds(0, BLOCK), pl.ds(2 * BLOCK, BLOCK)]
+        state = pair(
+            q2[p], [kv2[0, p, s, :] for s in sides], [kv2[1, p, s, :] for s in sides],
+            None, (i > 0, i < SEQ - 1), low_half, lo, hi,
+        )
+        for n in range(3):
+            st2[n, p] = state[n]
+
+    received(kv1.at[:, :, pl.ds(0, 128)], L1_P)
+    received(kv1.at[:, :, pl.ds(3 * BLOCK + 128, 128)], L1_N)
+
+    @pl.loop(0, 4)
+    def _(u):
+        b, p = lax.div(u, 2), lax.rem(u, 2)
+        own = pl.ds(pl.multiple_of(b * BLOCK, BLOCK), BLOCK)
+        sides = [own, pl.ds(pl.multiple_of((b + 2) * BLOCK, BLOCK), BLOCK)]
+        place = 2 * i + b
+        state = pair(
+            q1[p, own, :], [kv1[0, p, s, :] for s in sides], [kv1[1, p, s, :] for s in sides],
+            None, (place > 0, place < 2 * SEQ - 1), low_half, lo, hi,
+        )
+        for n in range(3):
+            st1[n, p, own, :] = state[n]
+
+    for p in range(2):
+        state = expand(tuple(st2[n, p] for n in range(3)), ex)
+        state = merge(state, tuple(st1[n, p] for n in range(3)))
+        for n in range(3):
+            st1[n, p] = state[n]
+
+    row = lax.broadcasted_iota(jnp.int32, (8, BLOCK), 0)
+
+    def finish(t):
+        d = lax.rem(t + HEADX - x, HEADX)
+        sums = []
+        for p in range(2):
+            coarse = expand(tuple(st1[n, p, pl.ds(pl.multiple_of(128 * t, 128), 128), :] for n in range(3)), ex)
+            fine = tuple(st0[n, p, pl.ds(pl.multiple_of(BLOCK * t, BLOCK), BLOCK), :] for n in range(3))
+            num, total, peak = merge(fine, coarse)
+            mean = (num / total).astype(BF16)
+            sums.append(jnp.transpose(peak + jnp.log(total)))
+            at[t, p] = mean
+
+            @pl.when(d == 0)
+            def _():
+                ra[x, p] = mean
+
+            @pl.when(d == 1)
+            def _():
+                send(at.at[t, p], ra.at[x, p], AT_L + p, i, x_up)
+
+            @pl.when(d == 3)
+            def _():
+                send(at.at[t, p], ra.at[x, p], AT_R + p, i, x_down)
+
+            @pl.when(d == 2)
+            def _():
+                send(at.at[t, p], via.at[p], VIA + p, i, x_down if p else x_up)
+
+        stat = jnp.where(row < 2, sums[0][0:8], sums[1][0:8])
+        stat = jnp.where(row == 1, sums[0][64:72], jnp.where(row == 3, sums[1][64:72], stat))
+        sstat[t] = stat
+
+        @pl.when(d == 0)
+        def _():
+            rstat[x] = stat
+
+        @pl.when(d > 0)
+        def _():
+            send(sstat.at[t], rstat.at[x], STAT + d, i, t)
+
+    finish(1)
+    finish(2)
 
     def one_head(ref, queries, place, count):
         tiles = [ref[n].reshape(BLOCK, 128) for n in range(2)]
@@ -326,52 +419,20 @@
     sends.append(send(rs3.at[1 - core], st3.at[core], RES3, sibling))
     st3[core] = rs3[core]
 
-    received(segi.at[0], SEG_P)
-    received(segi.at[2], SEG_N)
-    segf[pl.ds(0, 8), :] = segi[0].astype(F32)
-    segf[pl.ds(16, 8), :] = segi[2].astype(F32)
-    for side, (first, row1, row2) in enumerate(((0, 128, 192), (5 * BLOCK, 3 * BLOCK, 2 * BLOCK))):
-        received(kv0.at[:, :, pl.ds(first, BLOCK)], L0_P + side)
-        for n in range(2):
-            rim = jnp.concatenate([kv0[n, p, pl.ds(first, BLOCK), :] for p in range(2)], axis=1)
-            rim = jnp.dot(means[:192], rim, preferred_element_type=F32).astype(BF16)
-            for p in range(2):
-                kv1[n, p, pl.ds(row1, 128), :] = rim[:128, 128 * p : 128 * p + 128]
-                kv2[n, p, pl.ds(row2, 64), :] = rim[128:, 128 * p : 128 * p + 128]
-
-    received(kv2.at[:, :, pl.ds(0, 192)], L2_P)
-    received(kv2.at[:, :, pl.ds(2 * BLOCK + 64, 192)], L2_N)
-
-    @pl.loop(0, 2)
-    def _(p):
-        sides = [pl.ds(0, BLOCK), pl.ds(2 * BLOCK, BLOCK)]
-        state = pair(
-            q2[p], [kv2[0, p, s, :] for s in sides], [kv2[1, p, s, :] for s in sides],
-            None, (i > 0, i < SEQ - 1), low_half, lo, hi,
-        )
-        for n in range(3):
-            st2[n, p] = state[n]
-
-    received(kv1.at[:, :, pl.ds(0, 128)], L1_P)
-    received(kv1.at[:, :, pl.ds(3 * BLOCK + 128, 128)], L1_N)
-
-    @pl.loop(0, 4)
-    def _(u):
-        b, p = lax.div(u, 2), lax.rem(u, 2)
-        own = pl.ds(pl.multiple_of(b * BLOCK, BLOCK), BLOCK)
-        sides = [own, pl.ds(pl.multiple_of((b + 2) * BLOCK, BLOCK), BLOCK)]
-        place = 2 * i + b
-        state = pair(
-            q1[p, own, :], [kv1[0, p, s, :] for s in sides], [kv1[1, p, s, :] for s in sides],
-            None, (place > 0, place < 2 * SEQ - 1), low_half, lo, hi,
-        )
-        for n in range(3):
-            st1[n, p, own, :] = state[n]
-
     received(wbuf.at[x_far, quarter[0]], W2_L)
     received(wbuf.at[x_far, quarter[1]], W2_R)
     sends.append(send(wbuf.at[x_far, half], wbuf.at[x_far, half], W_ON_2, sibling))
 
+    first = jnp.where(x < 2, 3, 0)
+    for t in (first, 3 - first):
+        for p in range(2):
+            level0(t, p)
+        finish(t)
+    received(via.at[0], VIA)
+    sends.append(send(via.at[0], ra.at[x_down, 0], AT_2, i, x_up))
+    received(via.at[1], VIA + 1)
+    sends.append(send(via.at[1], ra.at[x_up, 1], AT_2 + 1, i, x_down))
+
     for d in range(1, 4):
         received(rrow4.at[lax.rem(a4 + 4 - d, 4)], RES4 + d)
 
@@ -384,6 +445,7 @@
         received(rrow5, RES5)
 
     received(st3.at[1 - core], RES3)
+    sums = []
     for p in range(2):
 
         def far(ref):
@@ -393,49 +455,26 @@
             return num, total, jnp.where(low_half, even[:, 32:33], odd[:, 32:33])
 
         state = merge(expand(far(rrow5), ex), far(rrow4))
-        state = merge(expand(state, ex), tuple(st3[p, n] for n in range(3)))
-        state = merge(expand(state, ex), tuple(st2[n, p] for n in range(3)))
-        state = merge(expand(state, ex), tuple(st1[n, p] for n in range(3)))
-        for n in range(3):
-            st1[n, p] = state[n]
-
-    def finish(t, p):
-        coarse = expand(tuple(st1[n, p, pl.ds(pl.multiple_of(128 * t, 128), 128), :] for n in range(3)), ex)
-        fine = tuple(st0[n, p, pl.ds(pl.multiple_of(BLOCK * t, BLOCK), BLOCK), :] for n in range(3))
-        num, total, _ = merge(fine, coarse)
-        attention = (num / total).astype(BF16)
-        d = lax.rem(t + HEADX - x, HEADX)
-        at[t, p] = attention
-
-        @pl.when(d == 0)
-        def _():
-            ra[x, p] = attention
-
-        @pl.when(d == 1)
-        def _():
-            send(at.at[t, p], ra.at[x, p], AT_L + p, i, x_up)
-
-        @pl.when(d == 3)
-        def _():
-            send(at.at[t, p], ra.at[x, p], AT_R + p, i, x_down)
-
-        @pl.when(d == 2)
-        def _():
-            send(at.at[t, p], via.at[p], VIA + p, i, x_down if p else x_up)
-
-    for t in (1, 2):
+        num, total, peak = merge(expand(state, ex), tuple(st3[p, n] for n in range(3)))
+        mean = num / total
+        sums.append(peak + jnp.log(total))
+        for t in range(4):
+            sfar[t, p] = mean[32 * t : 32 * t + 32]
+    both = jnp.where(lane < 96, pltpu.roll(sums[1], 64, 1), sums[1])
+    both = jnp.where(lane < 32, sums[0], jnp.where(low_half, pltpu.roll(sums[0], 96, 1), both))
+    for t in range(4):
+        sfar[t, 2] = both[32 * t : 32 * t + 32]
+    for d in (2, 1, 3):
+        other = lax.rem(x + d, HEADX)
+        sends.append(send(sfar.at[other], rfar.at[x], FAR + d, i, other))
+    rfar[x] = sfar[x]
+
+    for d in range(1, 4):
+        received(rstat.at[lax.rem(x + HEADX - d, HEADX)], STAT + d)
+    for m in range(4):
         for p in range(2):
-            finish(t, p)
-
-    first = jnp.where(x < 2, 3, 0)
-    for t in (first, 3 - first):
-        for p in range(2):
-            level0(t, p)
-            finish(t, p)
-    received(via.at[0], VIA)
-    sends.append(send(via.at[0], ra.at[x_down, 0], AT_2, i, x_up))
-    received(via.at[1], VIA + 1)
-    sends.append(send(via.at[1], ra.at[x_up, 1], AT_2 + 1, i, x_down))
+            lines = [jnp.broadcast_to(rstat[m, 2 * p + n : 2 * p + n + 1, :], (64, BLOCK)) for n in range(2)]
+            near[m, p] = jnp.transpose(jnp.concatenate(lines, axis=0))
 
     load_w.wait()
     other_half = pl.ds(128 * (1 - core), 128)
@@ -444,11 +483,24 @@
     for p in range(2):
         for owner, slot in ((x_down, AT_L), (x_up, AT_R), (x_far, AT_2)):
             received(ra.at[owner, p], slot + p)
+    for d in range(1, 4):
+        received(rfar.at[lax.rem(x + HEADX - d, HEADX)], FAR + d)
+
+    def spread(rows):
+        return jnp.broadcast_to(rows[:, None, :], (32, 8, 128)).reshape(BLOCK, 128)
+
+    attention = []
+    for m in range(4):
+        for p in range(2):
+            sums = jnp.where(low_half, rfar[m, 2, :, 64 * p : 64 * p + 1], rfar[m, 2, :, 64 * p + 32 : 64 * p + 33])
+            weight = 1.0 / (1.0 + jnp.exp(spread(sums) - near[m, p]))
+            coarse = spread(rfar[m, p])
+            attention.append((coarse + weight * (ra[m, p].astype(F32) - coarse)).astype(BF16))
     for n in range(4):
         columns = pl.ds(256 * n, 256)
         total = None
         for m in range(4):
-            rows = jnp.concatenate([ra[m, 0], ra[m, 1]], axis=1)
+            rows = jnp.concatenate(attention[2 * m : 2 * m + 2], axis=1)
             part = jnp.dot(rows, wbuf[m, :, columns], preferred_element_type=F32)
             total = part if total is None else total + part
         out_ref[:, columns] = total.astype(BF16)
@@ -472,6 +524,8 @@
     for p in range(2):
         for slot in (AT_L, AT_R, VIA):
             sent(at.at[0, p], slot + p)
+    for d in range(1, 4):
+        sent(sstat.at[0], STAT + d)
 
 
 def packed(first, second, h, low_half):
@@ -528,6 +582,11 @@
             vmem((4, 2, BLOCK, 128), BF16),
             vmem((4, 2, BLOCK, 128), BF16),
             vmem((2, BLOCK, 128), BF16),
+            vmem((4, 8, BLOCK), F32),
+            vmem((4, 8, BLOCK), F32),
+            vmem((4, 3, 32, 128), F32),
+            vmem((4, 3, 32, 128), F32),
+            vmem((4, 2, BLOCK, 128), F32),
             vmem((4, 256, 1024), BF16),
             pltpu.SemaphoreType.DMA((8,)),
             pltpu.SemaphoreType.DMA((N_SEM,)),

time: 49.5 us -> 48.7 us (0.984)
  Pallas kernels: 47.5 us -> 46.7 us
    pallas_call x1, Pallas kernels: 47.5 us -> 46.7 us  [on_device(): pl.pallas_call(kernel, out_shape=jax.ShapeDtypeStruct((BLOCK, 1024), BF16...]
where the time goes in v3:
time: 48.7 us; the launch traced here: 48.6 us
  Pallas kernels  46.7 us (96%)
  local copies, waits for them, and re-layouts  1.87 us (4%)
    pallas_call x1, Pallas kernels, on_device(): pl.pallas_call(kernel, out_shape=jax.ShapeDtypeStruct((BLOCK, 1024), BF16...  46.7 us
    unnamed x1, local copies, waits for them, and re-layouts  1.87 us

profile of v3, /device:TPU:1, one launch (start us, length us, event | category | flops | bytes accessed | tf_op | source)
XLA Modules:
  0.0 48.6 jit_solution(3033498803187772975)
XLA Ops:
  0.0 46.7 %block_attention.1 = bf16[256,1024]{1,0:T(8,128)(2,1)} custom-call(bf16[1024,256]{1,0:T(8,128)(2,1)} %q_hbm.1, bf16[1024,256]{1,0:T(8,128)(2,1)} %k_hbm.1, bf16[1024,256]{1,0:T(8,128)(2,1)} %v_hbm.1, s32[8,128]{1,0:T(8,128)} %bitcast.1, bf16[256,1024]{1,0:T(8,128)(2,1)} %w_hbm.1), custom_call_target="tpu_custom_call" | custom-call | tf_op jit(solution)/shard_map/block_attention/pallas_call | solution.py:546
  46.7 1.9 %copy.7 = bf16[256,1024]{1,0:T(8,128)(2,1)} copy(bf16[256,1024]{1,0:T(8,128)(2,1)} %block_attention.1) | data formatting | bytes 1048576

commit v4 on v3

--- a/solution.py
+++ b/solution.py
@@ -22,7 +22,8 @@
 W_L, W_R, W2_L, W2_R, W_ON_L, W_ON_R, W_ON_2 = range(22, 29)
 AT_L, AT_R, VIA, AT_2 = 29, 31, 33, 35
 STAT, FAR = 36, 39
-N_SEM = 43
+D3 = 43
+N_SEM = 44
 
 OWNER5 = (0, 1, 6, 7)
 
@@ -64,13 +65,34 @@
     return total, peak
 
 
-def pair(q, keys, values, biases, present, low_half, lo, hi):
-    even, even_peak = attend(q * lo, keys, [v * lo + hi for v in values], biases, present)
-    odd, odd_peak = attend(q * hi, keys, [v * hi + lo for v in values], biases, present)
-    num = jnp.where(low_half, even, odd)
-    total = pltpu.roll(jnp.where(low_half, odd, even), 64, 1)
-    peak = jnp.where(low_half, even_peak, odd_peak)
-    return num, total, peak
+def pairs(groups, low_half, lo, hi):
+    all_scores = []
+    for q, keys, _, biases, _ in groups:
+        q = jnp.concatenate([q * lo, q * hi], axis=0)
+        scores = [scores_of(q, k) for k in keys]
+        if biases is not None:
+            scores = [s + jnp.concatenate([b, b], axis=0) for s, b in zip(scores, biases)]
+        all_scores.append(scores)
+    ones = jnp.ones((BLOCK, 128), BF16)
+    results = []
+    for (q, _, values, _, present), scores in zip(groups, all_scores):
+        tops = [jnp.max(s, axis=1, keepdims=True) for s in scores]
+        if present is not None:
+            tops = [jnp.where(ok, t, NEG) for ok, t in zip(present, tops)]
+        peak = tops[0]
+        for t in tops[1:]:
+            peak = jnp.maximum(peak, t)
+        out = None
+        for index, (s, v) in enumerate(zip(scores, values)):
+            shift = peak if present is None else jnp.where(present[index], peak, BIG)
+            probs = jnp.exp(s - shift).astype(BF16)
+            part = jnp.dot(probs, jnp.concatenate([v, ones], axis=1), preferred_element_type=F32)
+            out = part if out is None else out + part
+        n = q.shape[0]
+        results.append(
+            tuple(jnp.where(low_half, w[:n], w[n:]) for w in (out[:, :128], out[:, 128:], peak))
+        )
+    return results
 
 
 def merge(a, b):
@@ -90,7 +112,7 @@
 def kernel(
     q_hbm, k_hbm, v_hbm, seg_hbm, w_hbm, out_ref,
     q0, kv0, segi, segf, q1, kv1, q2, kv2,
-    s3, r3, sq3, rq3, s4, r4, s5, r5, sq4, rq4, sq5, rq5,
+    s3, sd3, r3, sq3, rq3, s4, r4, s5, r5, sq4, rq4, sq5, rq5,
     st0, st1, st2, st3, rs3, srow4, rrow4, srow5, rrow5, ex, at, ra, via, sstat, rstat, sfar, rfar, near, wbuf,
     local, snd, rcv,
 ):
@@ -188,29 +210,34 @@
         first = 6 + 2 * (b + j)
         return [jnp.where(exists, segf[pl.ds(first + n, 1), :], -1.0) for n in range(2)]
 
-    def level0(b, p):
-        queries = q0[p, pl.ds(pl.multiple_of(b * BLOCK, BLOCK), BLOCK), :] * jnp.asarray(0.125, BF16)
+    def level0(b):
         own = [
             jnp.transpose(jnp.broadcast_to(segf[pl.ds(8 + 2 * b + n, 1), :], (128, 128))) for n in range(2)
         ]
         own = jnp.concatenate(own, axis=0)
-        keys, values, biases = [], [], []
-        for j in range(3):
-            rows = pl.ds(pl.multiple_of((b + j) * BLOCK, BLOCK), BLOCK)
-            keys.append(kv0[0, p, rows, :])
-            values.append(kv0[1, p, rows, :])
-            biases.append(
-                jnp.concatenate([jnp.where(own == near, 0.0, NEG) for near in bias_of(b, j)], axis=1)
+        biases = [
+            jnp.concatenate([jnp.where(own == near_by, 0.0, NEG) for near_by in bias_of(b, j)], axis=1) for j in range(3)
+        ]
+        here = pl.ds(pl.multiple_of(b * BLOCK, BLOCK), BLOCK)
+        rows = [pl.ds(pl.multiple_of((b + j) * BLOCK, BLOCK), BLOCK) for j in range(3)]
+        groups = [
+            (
+                q0[p, here, :] * jnp.asarray(0.125, BF16),
+                [kv0[0, p, r, :] for r in rows],
+                [kv0[1, p, r, :] for r in rows],
+                biases,
+                None,
             )
-        state = pair(queries, keys, values, biases, None, low_half, lo, hi)
-        for n in range(3):
-            st0[n, p, pl.ds(pl.multiple_of(b * BLOCK, BLOCK), BLOCK), :] = state[n]
+            for p in range(2)
+        ]
+        for p, state in enumerate(pairs(groups, low_half, lo, hi)):
+            for n in range(3):
+                st0[n, p, here, :] = state[n]
 
     @pl.when(late == 0)
     def _():
-        @pl.loop(0, 4)
-        def _(u):
-            level0(1 + lax.div(u, 2), lax.rem(u, 2))
+        level0(1)
+        level0(2)
 
     pl.semaphore_wait(barrier, 28)
     sends = []
@@ -249,30 +276,28 @@
         def _():
             rq5[a5] = sq5[h]
 
-    sends.append(send(segi.at[1], segi.at[0], SEG_P, right))
-    sends.append(send(segi.at[1], segi.at[2], SEG_N, left))
-    to_sides(kv0, ROWS, 0, L0_P)
-    to_sides(kv2, 256, 64, L2_P)
-    to_sides(kv1, 512, 128, L1_P)
     for direction, block in enumerate(blocks4):
         for j in range(4):
             send(s4.at[j], r4.at[direction, a4], KV4, block * 4 + j)
     for d in range(1, 4):
         other = lax.rem(a4 + d, 4)
         sends.append(send(sq4.at[other], rq4.at[a4], Q4 + d, g4 * 4 + other))
+    sends.append(send(segi.at[1], segi.at[0], SEG_P, right))
+    sends.append(send(segi.at[1], segi.at[2], SEG_N, left))
+    to_sides(kv0, ROWS, 0, L0_P)
+    to_sides(kv1, 512, 128, L1_P)
+    to_sides(kv2, 256, 128, L2_P)
     sends.append(send(sq3.at[1 - core], rq3.at[core], Q3, sibling))
-    for direction, by in enumerate((1, SEQ // 2 - 1)):
-        beside = lax.rem(chip + by, SEQ // 2)
-        for p in range(2):
-            send(s3.at[p], r3.at[direction, :, core], KV3, beside * 2 + p)
+    beside = lax.rem(chip + 1 + core * (SEQ // 2 - 2), SEQ // 2)
+    for p in range(2):
+        send(s3.at[p], r3.at[core, :, core], KV3, beside * 2 + p)
     rq3[core] = sq3[core]
     rq4[a4] = sq4[a4]
 
     @pl.when(late == 1)
     def _():
-        @pl.loop(0, 4)
-        def _(u):
-            level0(1 + lax.div(u, 2), lax.rem(u, 2))
+        level0(1)
+        level0(2)
 
     @pl.when(owner5)
     def _():
@@ -286,6 +311,30 @@
     received(wbuf.at[x_up, half], W_R)
     sends.append(send(wbuf.at[x_up, quarter[1]], wbuf.at[x_up, quarter[1]], W2_R, i, x_down))
     sends.append(send(wbuf.at[x_up, half], wbuf.at[x_up, half], W_ON_R, sibling))
+
+    def one_head(ref, queries, place, count):
+        tiles = [ref[n].reshape(BLOCK, 128) for n in range(2)]
+        out, peak = attend(queries, tiles, [t * hi + lo for t in tiles], None, (place > 0, place < count - 1))
+        return jnp.where((lane >= 32) & low_half, peak, out)
+
+    for d in range(1, 4):
+        received(rq4.at[lax.rem(a4 + 4 - d, 4)], Q4 + d)
+    received(r4, KV4)
+    srow4[...] = one_head(r4, rq4[...].reshape(BLOCK, 128), g4, SEQ // 4).reshape(4, 64, 128)
+    for d in range(1, 4):
+        other = lax.rem(a4 + d, 4)
+        sends.append(send(srow4.at[other], rrow4.at[a4], RES4 + d, g4 * 4 + other))
+    rrow4[a4] = srow4[a4]
+
+    @pl.when(owner5)
+    def _():
+        received(rq5.at[pl.ds(0, 7)], Q5)
+        received(r5.at[late], KV5_Y)
+        srow5[...] = one_head(r5, rq5[...].reshape(BLOCK, 128), g5, SEQ // 8).reshape(8, 32, 128)
+        for d in range(1, 8):
+            other = lax.rem(a5 + d, 8)
+            send(srow5.at[other], rrow5.at[head5], RES5, g5 * 8 + other)
+        rrow5[head5] = srow5[a5]
 
     received(segi.at[0], SEG_P)
     received(segi.at[2], SEG_N)
@@ -299,35 +348,43 @@
             for p in range(2):
                 kv1[n, p, pl.ds(row1, 128), :] = rim[:128, 128 * p : 128 * p + 128]
                 kv2[n, p, pl.ds(row2, 64), :] = rim[128:, 128 * p : 128 * p + 128]
-
-    received(kv2.at[:, :, pl.ds(0, 192)], L2_P)
-    received(kv2.at[:, :, pl.ds(2 * BLOCK + 64, 192)], L2_N)
-
-    @pl.loop(0, 2)
-    def _(p):
-        sides = [pl.ds(0, BLOCK), pl.ds(2 * BLOCK, BLOCK)]
-        state = pair(
-            q2[p], [kv2[0, p, s, :] for s in sides], [kv2[1, p, s, :] for s in sides],
-            None, (i > 0, i < SEQ - 1), low_half, lo, hi,
-        )
+    for side, (first, row2) in enumerate(((0, 128), (3 * BLOCK + 128, 2 * BLOCK + 64))):
+        received(kv1.at[:, :, pl.ds(first, 128)], L1_P + side)
+        for n in range(2):
+            rim = jnp.concatenate([kv1[n, p, pl.ds(first, 128), :] for p in range(2)], axis=1)
+            rim = jnp.dot(means[:64, :128], rim, preferred_element_type=F32).astype(BF16)
+            for p in range(2):
+                kv2[n, p, pl.ds(row2, 64), :] = rim[:, 128 * p : 128 * p + 128]
+
+    received(kv2.at[:, :, pl.ds(0, 128)], L2_P)
+    received(kv2.at[:, :, pl.ds(2 * BLOCK + 128, 128)], L2_N)
+
+    for n in range(2):
+        rows = pl.ds(pl.multiple_of(2 * BLOCK * core, BLOCK), BLOCK)
+        rim = jnp.concatenate([kv2[n, p, rows, :] for p in range(2)], axis=1)
+        rim = jnp.dot(means[:128], rim, preferred_element_type=F32).astype(BF16)
+        for p in range(2):
+            sd3[p, n] = rim[:, 128 * p : 128 * p + 128]
+    sends.append(send(sd3.at[1 - core], r3.at[core, :, 1 - core], D3, sibling))
+    r3[core, :, 1 - core] = sd3[core]
+
+    sides = [pl.ds(0, BLOCK), pl.ds(2 * BLOCK, BLOCK)]
+    present = (i > 0, i < SEQ - 1)
+    groups = [(q2[p], [kv2[0, p, r, :] for r in sides], [kv2[1, p, r, :] for r in sides], None, present) for p in range(2)]
+    for p, state in enumerate(pairs(groups, low_half, lo, hi)):
         for n in range(3):
             st2[n, p] = state[n]
-
-    received(kv1.at[:, :, pl.ds(0, 128)], L1_P)
-    received(kv1.at[:, :, pl.ds(3 * BLOCK + 128, 128)], L1_N)
-
-    @pl.loop(0, 4)
-    def _(u):
-        b, p = lax.div(u, 2), lax.rem(u, 2)
-        own = pl.ds(pl.multiple_of(b * BLOCK, BLOCK), BLOCK)
-        sides = [own, pl.ds(pl.multiple_of((b + 2) * BLOCK, BLOCK), BLOCK)]
-        place = 2 * i + b
-        state = pair(
-            q1[p, own, :], [kv1[0, p, s, :] for s in sides], [kv1[1, p, s, :] for s in sides],
-            None, (place > 0, place < 2 * SEQ - 1), low_half, lo, hi,
-        )
-        for n in range(3):
-            st1[n, p, own, :] = state[n]
+    for b in range(2):
+        own = pl.ds(b * BLOCK, BLOCK)
+        sides = [own, pl.ds((b + 2) * BLOCK, BLOCK)]
+        present = (2 * i + b > 0, 2 * i + b < 2 * SEQ - 1)
+        groups = [
+            (q1[p, own, :], [kv1[0, p, r, :] for r in sides], [kv1[1, p, r, :] for r in sides], None, present)
+            for p in range(2)
+        ]
+        for p, state in enumerate(pairs(groups, low_half, lo, hi)):
+            for n in range(3):
+                st1[n, p, own, :] = state[n]
 
     for p in range(2):
         state = expand(tuple(st2[n, p] for n in range(3)), ex)
@@ -379,40 +436,17 @@
     finish(1)
     finish(2)
 
-    def one_head(ref, queries, place, count):
-        tiles = [ref[n].reshape(BLOCK, 128) for n in range(2)]
-        out, peak = attend(queries, tiles, [t * hi + lo for t in tiles], None, (place > 0, place < count - 1))
-        return jnp.where((lane >= 32) & low_half, peak, out)
-
-    for d in range(1, 4):
-        received(rq4.at[lax.rem(a4 + 4 - d, 4)], Q4 + d)
-    received(r4, KV4)
-    srow4[...] = one_head(r4, rq4[...].reshape(BLOCK, 128), g4, SEQ // 4).reshape(4, 64, 128)
-    for d in range(1, 4):
-        other = lax.rem(a4 + d, 4)
-        sends.append(send(srow4.at[other], rrow4.at[a4], RES4 + d, g4 * 4 + other))
-    rrow4[a4] = srow4[a4]
-
-    @pl.when(owner5)
-    def _():
-        received(rq5.at[pl.ds(0, 7)], Q5)
-        received(r5.at[late], KV5_Y)
-        srow5[...] = one_head(r5, rq5[...].reshape(BLOCK, 128), g5, SEQ // 8).reshape(8, 32, 128)
-        for d in range(1, 8):
-            other = lax.rem(a5 + d, 8)
-            send(srow5.at[other], rrow5.at[head5], RES5, g5 * 8 + other)
-        rrow5[head5] = srow5[a5]
-
-    received(r3, KV3)
+    received(r3.at[0], KV3)
+    received(r3.at[1 - core, :, core], D3)
     received(rq3.at[1 - core], Q3)
-    state = pair(
+    group = (
         rq3[...].reshape(BLOCK, 128),
         [r3[n, 0].reshape(BLOCK, 128) for n in range(2)],
         [r3[n, 1].reshape(BLOCK, 128) for n in range(2)],
         None,
         (chip > 0, chip < SEQ // 2 - 1),
-        low_half, lo, hi,
     )
+    state = pairs([group], low_half, lo, hi)[0]
     for n in range(3):
         for m in range(2):
             rs3[m, n] = state[n][128 * m : 128 * m + 128]
@@ -425,8 +459,7 @@
 
     first = jnp.where(x < 2, 3, 0)
     for t in (first, 3 - first):
-        for p in range(2):
-            level0(t, p)
+        level0(t)
         finish(t)
     received(via.at[0], VIA)
     sends.append(send(via.at[0], ra.at[x_down, 0], AT_2, i, x_up))
@@ -520,7 +553,7 @@
         sent(srow5.at[pl.ds(0, 7)], RES5)
 
     sent(r4, KV4)
-    sent(r3, KV3)
+    sent(r3.at[0], KV3)
     for p in range(2):
         for slot in (AT_L, AT_R, VIA):
             sent(at.at[0, p], slot + p)
@@ -543,6 +576,7 @@
 
 def on_device(query_rows, key_rows, value_rows, segment, w_out):
     vmem = pltpu.VMEM
+    operands = (query_rows, key_rows, value_rows, segment.reshape(8, 128), w_out)
     return pl.pallas_call(
         kernel,
         out_shape=jax.ShapeDtypeStruct((BLOCK, 1024), BF16),
@@ -557,6 +591,7 @@
             vmem((2, 2, 1024, 128), BF16),
             vmem((2, 256, 128), BF16),
             vmem((2, 2, 768, 128), BF16),
+            vmem((2, 2, 128, 128), BF16),
             vmem((2, 2, 128, 128), BF16),
             vmem((2, 2, 2, 128, 128), BF16),
             vmem((2, 128, 128), BF16),
@@ -593,10 +628,10 @@
             pltpu.SemaphoreType.DMA((N_SEM,)),
         ],
         compiler_params=pltpu.CompilerParams(
-            collective_id=0, has_side_effects=True, vmem_limit_bytes=62 * 2**20
+            collective_id=0, has_side_effects=True, vmem_limit_bytes=48 * 2**20
         ),
         name="block_attention",
-    )(query_rows, key_rows, value_rows, segment.reshape(8, 128), w_out)
+    )(*[pltpu.with_memory_space_constraint(a, pltpu.HBM) for a in operands])
 
 
 def solution(mesh):

time: 48.7 us -> 44.6 us (0.916)
  Pallas kernels: 46.7 us -> 43.7 us
  local copies, waits for them, and re-layouts: 1.87 us -> 0.8 us
    pallas_call x1, Pallas kernels: 46.7 us -> 43.7 us  [on_device(): pl.pallas_call(kernel, out_shape=jax.ShapeDtypeStruct((BLOCK, 1024), BF16...]
    unnamed x1, local copies, waits for them, and re-layouts: 1.87 us -> 0.8 us
where the time goes in v4:
time: 44.6 us; the launch traced here: 44.5 us
  Pallas kernels  43.7 us (98%)
  local copies, waits for them, and re-layouts  0.8 us (2%)
    pallas_call x1, Pallas kernels, on_device(): pl.pallas_call(kernel, out_shape=jax.ShapeDtypeStruct((BLOCK, 1024), BF16...  43.7 us

profile of v4, /device:TPU:1, one launch (start us, length us, event | category | flops | bytes accessed | tf_op | source)
XLA Modules:
  0.0 44.5 jit_solution(2404418851859331074)
XLA Ops:
  0.0 43.7 %block_attention.1 = bf16[256,1024]{1,0:T(8,128)(2,1)S(1)} custom-call(bf16[1024,256]{1,0:T(8,128)(2,1)} %q_hbm.1, bf16[1024,256]{1,0:T(8,128)(2,1)} %k_hbm.1, bf16[1024,256]{1,0:T(8,128)(2,1)} %v_hbm.1, s32[8,128]{1,0:T(8,128)} %bitcast.1, bf16[256,1024]{1,0:T(8,128)(2,1)} %w_hbm.1), custom_call_target="tpu_custom_call" | custom-call | tf_op jit(solution)/shard_map/block_attention/pallas_call | solution.py:580
  43.7 0.8 %copy.7 = bf16[256,1024]{1,0:T(8,128)(2,1)} copy(bf16[256,1024]{1,0:T(8,128)(2,1)S(1)} %block_attention.1) | data formatting | bytes 1048576

commit v5 on v4

--- a/solution.py
+++ b/solution.py
@@ -276,17 +276,17 @@
         def _():
             rq5[a5] = sq5[h]
 
+    sends.append(send(segi.at[1], segi.at[0], SEG_P, right))
+    sends.append(send(segi.at[1], segi.at[2], SEG_N, left))
+    to_sides(kv0, ROWS, 0, L0_P)
+    to_sides(kv1, 512, 128, L1_P)
+    to_sides(kv2, 256, 128, L2_P)
     for direction, block in enumerate(blocks4):
         for j in range(4):
             send(s4.at[j], r4.at[direction, a4], KV4, block * 4 + j)
     for d in range(1, 4):
         other = lax.rem(a4 + d, 4)
         sends.append(send(sq4.at[other], rq4.at[a4], Q4 + d, g4 * 4 + other))
-    sends.append(send(segi.at[1], segi.at[0], SEG_P, right))
-    sends.append(send(segi.at[1], segi.at[2], SEG_N, left))
-    to_sides(kv0, ROWS, 0, L0_P)
-    to_sides(kv1, 512, 128, L1_P)
-    to_sides(kv2, 256, 128, L2_P)
     sends.append(send(sq3.at[1 - core], rq3.at[core], Q3, sibling))
     beside = lax.rem(chip + 1 + core * (SEQ // 2 - 2), SEQ // 2)
     for p in range(2):
@@ -315,26 +315,13 @@
     def one_head(ref, queries, place, count):
         tiles = [ref[n].reshape(BLOCK, 128) for n in range(2)]
         out, peak = attend(queries, tiles, [t * hi + lo for t in tiles], None, (place > 0, place < count - 1))
-        return jnp.where((lane >= 32) & low_half, peak, out)
-
-    for d in range(1, 4):
-        received(rq4.at[lax.rem(a4 + 4 - d, 4)], Q4 + d)
-    received(r4, KV4)
-    srow4[...] = one_head(r4, rq4[...].reshape(BLOCK, 128), g4, SEQ // 4).reshape(4, 64, 128)
-    for d in range(1, 4):
-        other = lax.rem(a4 + d, 4)
-        sends.append(send(srow4.at[other], rrow4.at[a4], RES4 + d, g4 * 4 + other))
-    rrow4[a4] = srow4[a4]
-
-    @pl.when(owner5)
-    def _():
-        received(rq5.at[pl.ds(0, 7)], Q5)
-        received(r5.at[late], KV5_Y)
-        srow5[...] = one_head(r5, rq5[...].reshape(BLOCK, 128), g5, SEQ // 8).reshape(8, 32, 128)
-        for d in range(1, 8):
-            other = lax.rem(a5 + d, 8)
-            send(srow5.at[other], rrow5.at[head5], RES5, g5 * 8 + other)
-        rrow5[head5] = srow5[a5]
+        sums = peak + jnp.log(jnp.where(low_half, out, 1.0))
+        first = sums.astype(BF16).astype(F32)
+        second = (sums - first).astype(BF16).astype(F32)
+        third = sums - first - second
+        mean = out / pltpu.roll(out, 64, 1)
+        parts = jnp.where(lane < 16, first, jnp.where(lane < 32, second, third))
+        return jnp.where(low_half, parts, mean).astype(BF16)
 
     received(segi.at[0], SEG_P)
     received(segi.at[2], SEG_N)
@@ -348,6 +335,9 @@
             for p in range(2):
                 kv1[n, p, pl.ds(row1, 128), :] = rim[:128, 128 * p : 128 * p + 128]
                 kv2[n, p, pl.ds(row2, 64), :] = rim[128:, 128 * p : 128 * p + 128]
+    level0(0)
+    level0(3)
+
     for side, (first, row2) in enumerate(((0, 128), (3 * BLOCK + 128, 2 * BLOCK + 64))):
         received(kv1.at[:, :, pl.ds(first, 128)], L1_P + side)
         for n in range(2):
@@ -392,10 +382,20 @@
         for n in range(3):
             st1[n, p] = state[n]
 
+    @pl.when(owner5)
+    def _():
+        received(rq5.at[pl.ds(0, 7)], Q5)
+        received(r5.at[late], KV5_Y)
+        srow5[...] = one_head(r5, rq5[...].reshape(BLOCK, 128), g5, SEQ // 8).reshape(8, 32, 128)
+        for d in range(1, 8):
+            other = lax.rem(a5 + d, 8)
+            send(srow5.at[other], rrow5.at[head5], RES5, g5 * 8 + other)
+        rrow5[head5] = srow5[a5]
+
     row = lax.broadcasted_iota(jnp.int32, (8, BLOCK), 0)
 
-    def finish(t):
-        d = lax.rem(t + HEADX - x, HEADX)
+    def finish(d):
+        t = lax.rem(x + d, HEADX)
         sums = []
         for p in range(2):
             coarse = expand(tuple(st1[n, p, pl.ds(pl.multiple_of(128 * t, 128), 128), :] for n in range(3)), ex)
@@ -403,38 +403,35 @@
             num, total, peak = merge(fine, coarse)
             mean = (num / total).astype(BF16)
             sums.append(jnp.transpose(peak + jnp.log(total)))
+            if d == 0:
+                ra[x, p] = mean
+                continue
             at[t, p] = mean
-
-            @pl.when(d == 0)
-            def _():
-                ra[x, p] = mean
-
-            @pl.when(d == 1)
-            def _():
-                send(at.at[t, p], ra.at[x, p], AT_L + p, i, x_up)
-
-            @pl.when(d == 3)
-            def _():
-                send(at.at[t, p], ra.at[x, p], AT_R + p, i, x_down)
-
-            @pl.when(d == 2)
-            def _():
-                send(at.at[t, p], via.at[p], VIA + p, i, x_down if p else x_up)
-
+            if d == 1:
+                sends.append(send(at.at[t, p], ra.at[x, p], AT_L + p, i, x_up))
+            if d == 3:
+                sends.append(send(at.at[t, p], ra.at[x, p], AT_R + p, i, x_down))
+            if d == 2:
+                sends.append(send(at.at[t, p], via.at[p], VIA + p, i, x_down if p else x_up))
         stat = jnp.where(row < 2, sums[0][0:8], sums[1][0:8])
         stat = jnp.where(row == 1, sums[0][64:72], jnp.where(row == 3, sums[1][64:72], stat))
-        sstat[t] = stat
-
-        @pl.when(d == 0)
-        def _():
+        if d == 0:
             rstat[x] = stat
-
-        @pl.when(d > 0)
-        def _():
-            send(sstat.at[t], rstat.at[x], STAT + d, i, t)
-
-    finish(1)
-    finish(2)
+        else:
+            sstat[t] = stat
+            sends.append(send(sstat.at[t], rstat.at[x], STAT + d, i, t))
+
+    for d in (2, 1, 3, 0):
+        finish(d)
+
+    for d in range(1, 4):
+        received(rq4.at[lax.rem(a4 + 4 - d, 4)], Q4 + d)
+    received(r4, KV4)
+    srow4[...] = one_head(r4, rq4[...].reshape(BLOCK, 128), g4, SEQ // 4).reshape(4, 64, 128)
+    for d in range(1, 4):
+        other = lax.rem(a4 + d, 4)
+        sends.append(send(srow4.at[other], rrow4.at[a4], RES4 + d, g4 * 4 + other))
+    rrow4[a4] = srow4[a4]
 
     received(r3.at[0], KV3)
     received(r3.at[1 - core, :, core], D3)
@@ -457,10 +454,6 @@
     received(wbuf.at[x_far, quarter[1]], W2_R)
     sends.append(send(wbuf.at[x_far, half], wbuf.at[x_far, half], W_ON_2, sibling))
 
-    first = jnp.where(x < 2, 3, 0)
-    for t in (first, 3 - first):
-        level0(t)
-        finish(t)
     received(via.at[0], VIA)
     sends.append(send(via.at[0], ra.at[x_down, 0], AT_2, i, x_up))
     received(via.at[1], VIA + 1)
@@ -482,10 +475,10 @@
     for p in range(2):
 
         def far(ref):
-            even, odd = ref[2 * p], ref[2 * p + 1]
+            even, odd = ref[2 * p].astype(F32), ref[2 * p + 1].astype(F32)
             num = jnp.where(low_half, pltpu.roll(even, 64, 1), odd)
-            total = jnp.where(low_half, even[:, 0:1], odd[:, 0:1])
-            return num, total, jnp.where(low_half, even[:, 32:33], odd[:, 32:33])
+            even, odd = [w[:, 0:1] + w[:, 16:17] + w[:, 32:33] for w in (even, odd)]
+            return num, jnp.ones_like(num), jnp.where(low_half, even, odd)
 
         state = merge(expand(far(rrow5), ex), far(rrow4))
         num, total, peak = merge(expand(state, ex), tuple(st3[p, n] for n in range(3)))
@@ -554,11 +547,6 @@
 
     sent(r4, KV4)
     sent(r3.at[0], KV3)
-    for p in range(2):
-        for slot in (AT_L, AT_R, VIA):
-            sent(at.at[0, p], slot + p)
-    for d in range(1, 4):
-        sent(sstat.at[0], STAT + d)
 
 
 def packed(first, second, h, low_half):
@@ -609,10 +597,10 @@
             vmem((3, 2, 256, 128), F32),
             vmem((2, 3, 128, 128), F32),
             vmem((2, 3, 128, 128), F32),
-            vmem((4, 64, 128), F32),
-            vmem((4, 64, 128), F32),
-            vmem((8, 32, 128), F32),
-            vmem((4, 32, 128), F32),
+            vmem((4, 64, 128), BF16),
+            vmem((4, 64, 128), BF16),
+            vmem((8, 32, 128), BF16),
+            vmem((4, 32, 128), BF16),
             vmem((3, 512, 128), F32),
             vmem((4, 2, BLOCK, 128), BF16),
             vmem((4, 2, BLOCK, 128), BF16),

time: 44.6 us -> 40.1 us (0.90)
  Pallas kernels: 43.7 us -> 39.2 us
    pallas_call x1, Pallas kernels: 43.7 us -> 39.2 us  [on_device(): pl.pallas_call(kernel, out_shape=jax.ShapeDtypeStruct((BLOCK, 1024), BF16...]
where the time goes in v5:
time: 40.1 us; the launch traced here: 40 us
  Pallas kernels  39.2 us (98%)
  local copies, waits for them, and re-layouts  0.8 us (2%)
    pallas_call x1, Pallas kernels, on_device(): pl.pallas_call(kernel, out_shape=jax.ShapeDtypeStruct((BLOCK, 1024), BF16...  39.2 us

profile of v5, /device:TPU:1, one launch (start us, length us, event | category | flops | bytes accessed | tf_op | source)
XLA Modules:
  0.0 40.0 jit_solution(15681885516117022478)
XLA Ops:
  0.0 39.2 %block_attention.1 = bf16[256,1024]{1,0:T(8,128)(2,1)S(1)} custom-call(bf16[1024,256]{1,0:T(8,128)(2,1)} %q_hbm.1, bf16[1024,256]{1,0:T(8,128)(2,1)} %k_hbm.1, bf16[1024,256]{1,0:T(8,128)(2,1)} %v_hbm.1, s32[8,128]{1,0:T(8,128)} %bitcast.1, bf16[256,1024]{1,0:T(8,128)(2,1)} %w_hbm.1), custom_call_target="tpu_custom_call" | custom-call | tf_op jit(solution)/shard_map/block_attention/pallas_call | solution.py:568
  39.2 0.8 %copy.7 = bf16[256,1024]{1,0:T(8,128)(2,1)} copy(bf16[256,1024]{1,0:T(8,128)(2,1)S(1)} %block_attention.1) | data formatting | bytes 1048576

commit v6 on v5

--- a/solution.py
+++ b/solution.py
@@ -304,14 +304,6 @@
         received(r5.at[1 - late], KV5)
         send(r5.at[1 - late], r5.at[late], KV5_Y, y_on)
 
-    quarter = [pl.ds(128 * core, 64), pl.ds(128 * core + 64, 64)]
-    received(wbuf.at[x_down, half], W_L)
-    sends.append(send(wbuf.at[x_down, quarter[0]], wbuf.at[x_down, quarter[0]], W2_L, i, x_up))
-    sends.append(send(wbuf.at[x_down, half], wbuf.at[x_down, half], W_ON_L, sibling))
-    received(wbuf.at[x_up, half], W_R)
-    sends.append(send(wbuf.at[x_up, quarter[1]], wbuf.at[x_up, quarter[1]], W2_R, i, x_down))
-    sends.append(send(wbuf.at[x_up, half], wbuf.at[x_up, half], W_ON_R, sibling))
-
     def one_head(ref, queries, place, count):
         tiles = [ref[n].reshape(BLOCK, 128) for n in range(2)]
         out, peak = attend(queries, tiles, [t * hi + lo for t in tiles], None, (place > 0, place < count - 1))
@@ -337,6 +329,14 @@
                 kv2[n, p, pl.ds(row2, 64), :] = rim[128:, 128 * p : 128 * p + 128]
     level0(0)
     level0(3)
+
+    quarter = [pl.ds(128 * core, 64), pl.ds(128 * core + 64, 64)]
+    received(wbuf.at[x_down, half], W_L)
+    sends.append(send(wbuf.at[x_down, quarter[0]], wbuf.at[x_down, quarter[0]], W2_L, i, x_up))
+    sends.append(send(wbuf.at[x_down, half], wbuf.at[x_down, half], W_ON_L, sibling))
+    received(wbuf.at[x_up, half], W_R)
+    sends.append(send(wbuf.at[x_up, quarter[1]], wbuf.at[x_up, quarter[1]], W2_R, i, x_down))
+    sends.append(send(wbuf.at[x_up, half], wbuf.at[x_up, half], W_ON_R, sibling))
 
     for side, (first, row2) in enumerate(((0, 128), (3 * BLOCK + 128, 2 * BLOCK + 64))):
         received(kv1.at[:, :, pl.ds(first, 128)], L1_P + side)
@@ -485,9 +485,13 @@
         mean = num / total
         sums.append(peak + jnp.log(total))
         for t in range(4):
-            sfar[t, p] = mean[32 * t : 32 * t + 32]
+            sfar[t, p] = mean[32 * t : 32 * t + 32].astype(BF16)
     both = jnp.where(lane < 96, pltpu.roll(sums[1], 64, 1), sums[1])
     both = jnp.where(lane < 32, sums[0], jnp.where(low_half, pltpu.roll(sums[0], 96, 1), both))
+    high = both.astype(BF16).astype(F32)
+    middle = (both - high).astype(BF16).astype(F32)
+    place = lax.rem(lane, 32)
+    both = jnp.where(place < 8, high, jnp.where(place < 16, middle, both - high - middle)).astype(BF16)
     for t in range(4):
         sfar[t, 2] = both[32 * t : 32 * t + 32]
     for d in (2, 1, 3):
@@ -518,9 +522,13 @@
     attention = []
     for m in range(4):
         for p in range(2):
-            sums = jnp.where(low_half, rfar[m, 2, :, 64 * p : 64 * p + 1], rfar[m, 2, :, 64 * p + 32 : 64 * p + 33])
+            parts = rfar[m, 2].astype(F32)
+            even, odd = [
+                parts[:, n : n + 1] + parts[:, n + 8 : n + 9] + parts[:, n + 16 : n + 17] for n in (64 * p, 64 * p + 32)
+            ]
+            sums = jnp.where(low_half, even, odd)
             weight = 1.0 / (1.0 + jnp.exp(spread(sums) - near[m, p]))
-            coarse = spread(rfar[m, p])
+            coarse = spread(rfar[m, p].astype(F32))
             attention.append((coarse + weight * (ra[m, p].astype(F32) - coarse)).astype(BF16))
     for n in range(4):
         columns = pl.ds(256 * n, 256)
@@ -607,8 +615,8 @@
             vmem((2, BLOCK, 128), BF16),
             vmem((4, 8, BLOCK), F32),
             vmem((4, 8, BLOCK), F32),
-            vmem((4, 3, 32, 128), F32),
-            vmem((4, 3, 32, 128), F32),
+            vmem((4, 3, 32, 128), BF16),
+            vmem((4, 3, 32, 128), BF16),
             vmem((4, 2, BLOCK, 128), F32),
             vmem((4, 256, 1024), BF16),
             pltpu.SemaphoreType.DMA((8,)),

time: 40.1 us -> 39.1 us (0.975)
  Pallas kernels: 39.2 us -> 38.2 us
    pallas_call x1, Pallas kernels: 39.2 us -> 38.2 us  [on_device(): pl.pallas_call(kernel, out_shape=jax.ShapeDtypeStruct((BLOCK, 1024), BF16...]
where the time goes in v6:
time: 39.1 us; the launch traced here: 39 us
  Pallas kernels  38.2 us (98%)
  local copies, waits for them, and re-layouts  0.8 us (2%)
    pallas_call x1, Pallas kernels, on_device(): pl.pallas_call(kernel, out_shape=jax.ShapeDtypeStruct((BLOCK, 1024), BF16...  38.2 us
    unnamed x1, local copies, waits for them, and re-layouts  0.8 us

profile of v6, /device:TPU:1, one launch (start us, length us, event | category | flops | bytes accessed | tf_op | source)
XLA Modules:
  0.0 39.0 jit_solution(12818821729470272429)
XLA Ops:
  0.0 38.2 %block_attention.1 = bf16[256,1024]{1,0:T(8,128)(2,1)S(1)} custom-call(bf16[1024,256]{1,0:T(8,128)(2,1)} %q_hbm.1, bf16[1024,256]{1,0:T(8,128)(2,1)} %k_hbm.1, bf16[1024,256]{1,0:T(8,128)(2,1)} %v_hbm.1, s32[8,128]{1,0:T(8,128)} %bitcast.1, bf16[256,1024]{1,0:T(8,128)(2,1)} %w_hbm.1), custom_call_target="tpu_custom_call" | custom-call | tf_op jit(solution)/shard_map/block_attention/pallas_call | solution.py:576
  38.2 0.8 %copy.7 = bf16[256,1024]{1,0:T(8,128)(2,1)} copy(bf16[256,1024]{1,0:T(8,128)(2,1)S(1)} %block_attention.1) | data formatting | bytes 1048576

commit v7 on v6

--- a/solution.py
+++ b/solution.py
@@ -609,7 +609,7 @@
             vmem((4, 64, 128), BF16),
             vmem((8, 32, 128), BF16),
             vmem((4, 32, 128), BF16),
-            vmem((3, 512, 128), F32),
+            vmem((3, 520, 128), F32),
             vmem((4, 2, BLOCK, 128), BF16),
             vmem((4, 2, BLOCK, 128), BF16),
             vmem((2, BLOCK, 128), BF16),

time: 39.1 us -> 39.1 us (level)
  no operation moved by 1% of the time
where the time goes in v7:
time: 39.1 us; the launch traced here: 39 us
  Pallas kernels  38.2 us (98%)
  local copies, waits for them, and re-layouts  0.8 us (2%)
    pallas_call x1, Pallas kernels, on_device(): pl.pallas_call(kernel, out_shape=jax.ShapeDtypeStruct((BLOCK, 1024), BF16...  38.2 us
    unnamed x1, local copies, waits for them, and re-layouts  0.8 us

profile of v7, /device:TPU:1, one launch (start us, length us, event | category | flops | bytes accessed | tf_op | source)
XLA Modules:
  0.0 39.0 jit_solution(10104193733110144611)
XLA Ops:
  0.0 38.2 %block_attention.1 = bf16[256,1024]{1,0:T(8,128)(2,1)S(1)} custom-call(bf16[1024,256]{1,0:T(8,128)(2,1)} %q_hbm.1, bf16[1024,256]{1,0:T(8,128)(2,1)} %k_hbm.1, bf16[1024,256]{1,0:T(8,128)(2,1)} %v_hbm.1, s32[8,128]{1,0:T(8,128)} %bitcast.1, bf16[256,1024]{1,0:T(8,128)(2,1)} %w_hbm.1), custom_call_target="tpu_custom_call" | custom-call | tf_op jit(solution)/shard_map/block_attention/pallas_call | solution.py:576
  38.2 0.8 %copy.7 = bf16[256,1024]{1,0:T(8,128)(2,1)} copy(bf16[256,1024]{1,0:T(8,128)(2,1)S(1)} %block_attention.1) | data formatting | bytes 1048576
